TPU v7x, 256 devices: a whole 4x4x8 slice. The times are simulated.
256 devices in a mesh: dp: 32 (over x, z), ctx: 8 (over y, core).
Axes of the slice: x: 4, y: 4, z: 8, core: 2. Of those that a mesh axis runs over, the one named last changes fastest.
Arguments:
- inputs: bfloat16 [32, 1024, 2048], P('dp', 'ctx'), may hold values from -12 to 12
- doc_ids: int32 [32, 1024], P('dp', 'ctx'), may hold values from 0 to 3, never falling along the last dimension, each value on 1 to 512 neighbouring positions
- dilation: int32 [1], replicated, may hold values from 1 to 256
- filter_w: bfloat16 [2, 2048, 2048], P(None, 'dp', 'ctx'), may hold values from -0.09375 to 0.09375
- gate_w: bfloat16 [2, 2048, 2048], P(None, 'dp', 'ctx'), may hold values from -0.09375 to 0.09375
- filter_m: float32 [2, 2048, 2048], P(None, 'dp', 'ctx'), may hold values from -0.01171875 to 0.01171875
- filter_v: float32 [2, 2048, 2048], P(None, 'dp', 'ctx'), may hold values from 1e-07 to 4e-06
- gate_m: float32 [2, 2048, 2048], P(None, 'dp', 'ctx'), may hold values from -0.01171875 to 0.01171875
- gate_v: float32 [2, 2048, 2048], P(None, 'dp', 'ctx'), may hold values from 1e-07 to 4e-06
- cotangent: bfloat16 [32, 1024, 2048], P('dp', 'ctx'), may hold values from -6 to 6
Outputs:
- layer_out: bfloat16 [32, 1024, 2048], P('dp', 'ctx')
- input_grad: bfloat16 [32, 1024, 2048], P('dp', 'ctx')
- new_filter_w: bfloat16 [2, 2048, 2048], P(None, 'dp', 'ctx')
- new_gate_w: bfloat16 [2, 2048, 2048], P(None, 'dp', 'ctx')
- new_filter_m: float32 [2, 2048, 2048], P(None, 'dp', 'ctx')
- new_filter_v: float32 [2, 2048, 2048], P(None, 'dp', 'ctx')
- new_gate_m: float32 [2, 2048, 2048], P(None, 'dp', 'ctx')
- new_gate_v: float32 [2, 2048, 2048], P(None, 'dp', 'ctx')
Inputs may be any that keep to these rules, and one draw needn't show every extreme that they name: `doc_ids`: document numbers never fall along a sequence; a document covers at most 512 positions.
All inputs are finite; a program needn't handle non-finite values.
Results may differ from a plain program's by a relative error of at most 0.0075.
Values may be sent and summed in bfloat16 or wider, within the bound.
A program may use at most 128 MiB of HBM per device.

v0:
```python
import jax
import jax.numpy as jnp
from jax import lax
from jax.sharding import Mesh
from jax.sharding import PartitionSpec as P

STEP = 10
CTX = ("ctx_0", "ctx_1")
DP = ("dp_0", "dp_1")


BETA_ONE = 0.9
BETA_TWO = 0.95
LEARN_RATE = 0.001
EPSILON = 1e-08


def copy_for_each(array, axis):
    length = lax.axis_size(axis)
    return lax.all_to_all(
        jnp.broadcast_to(array[None], (length, *array.shape)), axis, 0, 0, tiled=True
    )


def laid_out(pieces, dim):
    pieces = jnp.moveaxis(pieces, 0, dim)
    shape = pieces.shape
    return pieces.reshape(*shape[:dim], shape[dim] * shape[dim + 1], *shape[dim + 2 :])


def gathered_by_axis(array, axes, dim):
    far, near = axes
    leading = copy_for_each(array, far)
    pieces = jnp.swapaxes(copy_for_each(leading, near), 0, 1)
    return laid_out(pieces.reshape(-1, *array.shape), dim)


def sent_together(arrays, axis, dim, along):
    ends, at = ([], 0)
    for a in arrays[:-1]:
        at += a.shape[along]
        ends.append(at)
    both = jnp.concatenate(arrays, axis=along)
    return tuple(jnp.split(lax.all_gather(both, axis, axis=dim, tiled=True), ends, axis=along))


def split_up(array, dim, length):
    shape = array.shape
    pieces = array.reshape(*shape[:dim], length, shape[dim] // length, *shape[dim + 1 :])
    return jnp.moveaxis(pieces, dim, 0)


def sum_at_owner(array, axis, dim):
    length = lax.axis_size(axis)
    pieces = lax.all_to_all(split_up(array, dim, length), axis, 0, 0, tiled=True)
    return jnp.sum(pieces.astype(jnp.float32), axis=0)


def sum_in_two_steps(array, axes, dim):
    far, near = axes
    pieces = split_up(array, dim, lax.axis_size(far))
    nearer = sum_at_owner(pieces, near, dim + 1)
    arrived = lax.all_to_all(
        nearer.astype(jnp.bfloat16), far, split_axis=0, concat_axis=0, tiled=True
    )
    return arrived.astype(jnp.float32).sum(axis=0)


def sum_by_axis(so_far, axes):
    for axis in axes:
        so_far = lax.psum_scatter(so_far, axis, scatter_dimension=0, tiled=True)
    return so_far


def lagged_rows(sequence, seq_ids, shift_by):
    length = sequence.shape[0]
    start_row = length - shift_by
    padded = jnp.concatenate([jnp.zeros_like(sequence), sequence], axis=0)
    shifted = lax.dynamic_slice_in_dim(padded, start_row, length, 0)
    id_padded = jnp.concatenate([jnp.full((length,), -1, jnp.int32), seq_ids], axis=0)
    id_shifted = lax.dynamic_slice_in_dim(id_padded, start_row, length, 0)
    return jnp.where((id_shifted == seq_ids)[:, None], shifted, jnp.zeros_like(shifted))


def adam_update(weight, moment, second, gradient):
    new_moment = BETA_ONE * moment + (1.0 - BETA_ONE) * gradient
    new_second = BETA_TWO * second + (1.0 - BETA_TWO) * gradient * gradient
    first_fix = 1.0 - BETA_ONE**STEP
    second_fix = 1.0 - BETA_TWO**STEP
    step_size = new_moment / first_fix / (jnp.sqrt(new_second / second_fix) + EPSILON)
    new_weight = (weight.astype(jnp.float32) - LEARN_RATE * step_size).astype(jnp.bfloat16)
    return (new_weight, new_moment, new_second)


def per_device(
    inputs, doc_ids, dilation, filter_w, gate_w, filter_m, filter_v, gate_m, gate_v, cotangent
):
    gathered, gathered_ids = (
        gathered_by_axis(inputs, ("ctx_0", "ctx_1"), 1),
        gathered_by_axis(doc_ids, ("ctx_0", "ctx_1"), 1),
    )
    sequence = gathered[0]
    seq_ids = gathered_ids[0]
    shift_by = dilation[0]
    lagged = lagged_rows(sequence, seq_ids, shift_by)
    length = sequence.shape[0]
    columns = filter_w.shape[2]
    held_filter, held_gate = sent_together((filter_w, gate_w), DP, 1, 0)
    first_tap = jnp.concatenate([held_filter[0], held_gate[0]], axis=1)
    second_tap = jnp.concatenate([held_filter[1], held_gate[1]], axis=1)
    pre_act = jnp.dot(sequence, first_tap, preferred_element_type=jnp.float32) + jnp.dot(
        lagged, second_tap, preferred_element_type=jnp.float32
    )
    filter_tanh = jnp.tanh(pre_act[:, :columns])
    gate_sigmoid = jax.nn.sigmoid(pre_act[:, columns:])
    gated_cols = (filter_tanh * gate_sigmoid).astype(jnp.bfloat16)
    gated_rows = lax.all_to_all(gated_cols, CTX, split_axis=0, concat_axis=1, tiled=True)
    layer_out = (inputs[0].astype(jnp.float32) + gated_rows.astype(jnp.float32)).astype(
        jnp.bfloat16
    )
    cot_cols = lax.all_to_all(cotangent[0], CTX, split_axis=1, concat_axis=0, tiled=True)
    cot_float = cot_cols.astype(jnp.float32)
    filter_delta = (cot_float * gate_sigmoid * (1.0 - filter_tanh * filter_tanh)).astype(
        jnp.bfloat16
    )
    gate_delta = (cot_float * filter_tanh * gate_sigmoid * (1.0 - gate_sigmoid)).astype(
        jnp.bfloat16
    )
    pre_grad = jnp.concatenate([filter_delta, gate_delta], axis=1)
    back_filter, back_gate = (held_filter, held_gate)
    back_zero = jnp.concatenate([back_filter[0], back_gate[0]], axis=1)
    back_one = jnp.concatenate([back_filter[1], back_gate[1]], axis=1)
    ahead_grad = jnp.concatenate([pre_grad, jnp.zeros_like(pre_grad)], axis=0)
    ahead_ids = jnp.concatenate([seq_ids, jnp.full((length,), -1, jnp.int32)], axis=0)
    row_count = cotangent.shape[1] * lax.axis_size(CTX)
    rows_ahead = lax.dynamic_slice_in_dim(ahead_grad, shift_by, row_count, 0)
    ids_later = lax.dynamic_slice_in_dim(ahead_ids, shift_by, row_count, 0)
    near_term = lax.dot_general(
        pre_grad, back_zero, (((1,), (1,)), ((), ())), preferred_element_type=jnp.float32
    )
    far_term = lax.dot_general(
        rows_ahead, back_one, (((1,), (1,)), ((), ())), preferred_element_type=jnp.float32
    )
    input_sum = sum_in_two_steps(
        (
            near_term
            + jnp.where((ids_later == seq_ids)[:, None], far_term, jnp.zeros_like(far_term))
        ).astype(jnp.bfloat16),
        ("ctx_0", "ctx_1"),
        0,
    )
    input_grad = (cotangent[0].astype(jnp.float32) + input_sum).astype(jnp.bfloat16)
    grad_zero = lax.dot_general(
        sequence, pre_grad, (((0,), (0,)), ((), ())), preferred_element_type=jnp.float32
    )
    grad_one = lax.dot_general(
        lagged, pre_grad, (((0,), (0,)), ((), ())), preferred_element_type=jnp.float32
    )
    summed = sum_by_axis(jnp.stack([grad_zero, grad_one], axis=1), DP)
    tokens_all = length * lax.axis_size(DP)
    filter_grad = jnp.transpose(summed[:, :, :columns], (1, 0, 2)) / tokens_all
    gate_grad = jnp.transpose(summed[:, :, columns:], (1, 0, 2)) / tokens_all
    new_filter_w, new_filter_m, new_filter_v = adam_update(
        filter_w, filter_m, filter_v, filter_grad
    )
    new_gate_w, new_gate_m, new_gate_v = adam_update(gate_w, gate_m, gate_v, gate_grad)
    return (
        layer_out[None],
        input_grad[None],
        new_filter_w,
        new_gate_w,
        new_filter_m,
        new_filter_v,
        new_gate_m,
        new_gate_v,
    )


def solution(mesh):
    torus = Mesh(mesh.devices.reshape(4, 8, 4, 2), ("dp_0", "dp_1", "ctx_0", "ctx_1"))
    placed = (
        P(DP, CTX, None),
        P(DP, CTX),
        P(),
        P(None, DP, CTX),
        P(None, DP, CTX),
        P(None, DP, CTX),
        P(None, DP, CTX),
        P(None, DP, CTX),
        P(None, DP, CTX),
        P(DP, CTX, None),
    )
    return jax.shard_map(
        per_device,
        mesh=torus,
        in_specs=placed,
        out_specs=(
            P(DP, CTX, None),
            P(DP, CTX, None),
            P(None, DP, CTX),
            P(None, DP, CTX),
            P(None, DP, CTX),
            P(None, DP, CTX),
            P(None, DP, CTX),
            P(None, DP, CTX),
        ),
        check_vma=False,
    )
```

profile of v0, /device:TPU:2, one launch (start us, length us, event | category | flops | bytes accessed | tf_op | source)
XLA Modules:
  0.0 291.7 jit_solution(1879403617857947221)
XLA Ops:
  7.2 1.6 pad_maximum_fusion.8
  8.8 0.7 broadcast_in_dim.61
  9.5 9.5 %all_to_all.56 = s32[4,1,128]{2,1,0:T(1,128)S(1)} all-to-all(s32[4,1,128]{2,1,0:T(1,128)S(1)} %broadcast_in_dim.61), channel_id=1, replica_groups=mesh['dp_0'=4,'dp_1'=8,'ctx_0'=4,'ctx_1'=2] {'ctx_0'}, dimensions={0} | all-to-all | bytes 4096 | tf_op jit(solution)/shard_map/all_to_all | solution.py:20
  19.0 3.7 %all_to_all.57 = s32[2,4,1,128]{3,1,2,0:T(4,128)S(1)} all-to-all(s32[2,4,1,128]{3,1,2,0:T(4,128)S(1)} %broadcast_in_dim.63), channel_id=1, replica_groups=mesh['dp_0'=4,'dp_1'=8,'ctx_0'=4,'ctx_1'=2] {'ctx_1'}, dimensions={0} | all-to-all | bytes 8192 | tf_op jit(solution)/shard_map/all_to_all | solution.py:20
  22.7 2.7 broadcast_in_dim.57
  25.3 3.6 %all-to-all-start = ((bf16[4,1,128,2048]{3,2,1,0:T(8,128)(2,1)}), bf16[4,1,128,2048]{3,2,1,0:T(8,128)(2,1)S(1)}, u32[]{:S(2)}, u32[]{:S(2)}) async-start(bf16[4,1,128,2048]{3,2,1,0:T(8,128)(2,1)} %broadcast_in_dim.57), calls=%async_computation | async-start | bytes 4194304 | tf_op jit(solution)/shard_map/all_to_all | solution.py:20
  29.6 1.0 copy.99
  30.6 0.1 fusion.16
  30.7 25.2 %all-to-all-done = bf16[4,1,128,2048]{3,2,1,0:T(8,128)(2,1)S(1)} async-done(((bf16[4,1,128,2048]{3,2,1,0:T(8,128)(2,1)}), bf16[4,1,128,2048]{3,2,1,0:T(8,128)(2,1)S(1)}, u32[]{:S(2)}, u32[]{:S(2)}) %all-to-all-start) | async-done | bytes 2097184 | tf_op jit(solution)/shard_map/all_to_all | solution.py:20
  55.9 0.5 broadcast_in_dim.59
  56.4 8.2 %all_to_all.58 = bf16[2,4,1,128,2048]{4,3,1,2,0:T(8,128)(2,1)} all-to-all(bf16[2,4,1,128,2048]{4,3,1,2,0:T(8,128)(2,1)S(1)} %broadcast_in_dim.59), channel_id=1, replica_groups=mesh['dp_0'=4,'dp_1'=8,'ctx_0'=4,'ctx_1'=2] {'ctx_1'}, dimensions={0} | all-to-all | bytes 8388608 | tf_op jit(solution)/shard_map/all_to_all | solution.py:20
  64.6 3.5 %all-to-all-start.5 = ((bf16[128,8,256]{0,2,1:T(8,128)(2,1)}), bf16[128,8,256]{0,2,1:T(8,128)(2,1)S(1)}, u32[]{:S(2)}, u32[]{:S(2)}) async-start(bf16[128,8,256]{0,2,1:T(8,128)(2,1)} %bitcast.17), calls=%async_computation.5 | async-start | bytes 1048576 | tf_op jit(solution)/shard_map/all_to_all | solution.py:121
  68.1 4.8 %copy.94 = bf16[2,4,1,128,2048]{4,3,0,1,2:T(8,128)(2,1)} copy(bf16[2,4,1,128,2048]{4,3,1,2,0:T(8,128)(2,1)} %all_to_all.58) | data formatting | bytes 8388608 | tf_op jit(solution)/shard_map/all_to_all | solution.py:20
  72.9 21.7 %all-gather.2.cloned.1.call-done = bf16[4,2048,256]{2,1,0:T(8,128)(2,1)} async-done(((bf16[4,64,256]{2,1,0:T(8,128)(2,1)}), bf16[4,2048,256]{2,1,0:T(8,128)(2,1)}) %all-gather.2.cloned.1.call-update) | async-done | bytes 4194320 | tf_op jit(solution)/shard_map/all_gather | solution.py:44
  94.7 2.6 slice_bitcast_fusion.3
  97.3 0.8 copy-done
  98.1 3.1 %fusion.1 = f32[1024,512]{0,1:T(8,128)S(1)} fusion(bf16[2048,256]{1,0:T(8,128)(2,1)S(1)} %get-tuple-element.47, bf16[2048,256]{1,0:T(8,128)(2,1)S(1)} %get-tuple-element.48, s32[]{:T(128)S(6)} %select_n.16, bf16[1024,2048]{1,0:T(8,128)(2,1)S(1)} %bitcast.82, pred[1024]{0:T(1024)(128)(4,1)S(1)} %get-tuple-element.56), kind=kOutput, calls=%fused_computation.12 | convolution fusion | flops 2153775104 | bytes 8389636 | tf_op jit(solution)/shard_map/dot_general | solution.py:111
  101.3 2.4 bitcast_add_fusion
  103.7 0.7 fusion.4
  104.4 1.8 copy-done.1
  106.2 2.7 convolution_bitcast_fusion
  109.0 2.4 convolution_bitcast_fusion.1
  111.4 3.9 %pad_maximum_fusion = f32[2048,2,512]{0,2,1:T(8,128)} fusion(f32[2048,1,512]{0,2,1:T(8,128)S(1)} %convolution_bitcast_fusion, f32[2048,1,512]{0,2,1:T(8,128)S(1)} %convolution_bitcast_fusion.1), kind=kLoop, calls=%fused_computation | loop fusion | flops 2097152 | bytes 16777216 | tf_op jit(solution)/shard_map/stack | solution.py:159
  115.2 0.9 copy.125
  116.1 0.1 copy-done.6
  116.3 0.3 copy-done.8
  116.6 0.1 pad_maximum_fusion.7
  116.7 0.3 copy-done.14
  117.0 4.0 %fusion.2 = f32[1024,2048]{1,0:T(8,128)S(1)} fusion(bf16[2048,256]{1,0:T(8,128)(2,1)} %copy-done.15, bf16[2048,256]{1,0:T(8,128)(2,1)S(1)} %copy-done.14, bf16[1024,256]{0,1:T(8,128)(2,1)S(1)} %copy-done.8, bf16[1024,256]{0,1:T(8,128)(2,1)S(1)} %copy-done.6), kind=kOutput, calls=%fused_computation.13 | convolution fusion | flops 2153775104 | bytes 11534336 | tf_op jit(solution)/shard_map/dot_general | solution.py:138
  121.0 4.2 %add_convert_fusion = bf16[1024,2048]{1,0:T(8,128)(2,1)S(1)} fusion(f32[1024,2048]{1,0:T(8,128)S(1)} %fusion.2, pred[1024]{0:T(1024)(128)(4,1)S(1)} %get-tuple-element.55, bf16[2048,256]{1,0:T(8,128)(2,1)S(1)} %copy-done.10, bf16[2048,256]{1,0:T(8,128)(2,1)S(1)} %copy-done.12, s32[]{:T(128)S(6)} %select_n.18, bf16[1024,512]{0,1:T(8,128)(2,1)S(1)} %pad_maximum_fusion.7), kind=kOutput, calls=%fused_computation.1 | convolution fusion | flops 2157969408 | bytes 15729668 | tf_op jit(solution)/shard_map/dot_general | solution.py:141
  125.2 0.3 copy.124
  125.5 8.2 %all_to_all.59 = bf16[2,4,128,2048]{3,2,1,0:T(8,128)(2,1)} all-to-all(bf16[2,4,128,2048]{3,2,1,0:T(8,128)(2,1)S(1)} %bitcast.80), channel_id=1, replica_groups=mesh['dp_0'=4,'dp_1'=8,'ctx_0'=4,'ctx_1'=2] {'ctx_1'}, dimensions={0} | all-to-all | bytes 8388608 | tf_op jit(solution)/shard_map/all_to_all | solution.py:55
  133.7 4.3 %all-to-all-start.4 = ((bf16[8,128,256]{1,2,0:T(8,128)(2,1)}), bf16[8,128,256]{1,2,0:T(8,128)(2,1)S(1)}, u32[]{:S(2)}, u32[]{:S(2)}) async-start(bf16[8,128,256]{1,2,0:T(8,128)(2,1)} %bitcast.74), calls=%async_computation.4 | async-start | bytes 1048576 | tf_op jit(solution)/shard_map/all_to_all | solution.py:117
  137.9 5.1 %reduce_sum.23 = bf16[4,128,2048]{2,1,0:T(8,128)(2,1)} reduce(bf16[2,4,128,2048]{3,2,1,0:T(8,128)(2,1)} %all_to_all.59, bf16[]{:T(256)} %constant.15.clone.1), dimensions={0}, to_apply=%region_0.1 | reduce | flops 1048576 | bytes 6291458 | tf_op jit(solution)/shard_map/reduce_sum | solution.py:56
  143.0 5.3 %all-to-all-done.4 = bf16[8,128,256]{1,2,0:T(8,128)(2,1)S(1)} async-done(((bf16[8,128,256]{1,2,0:T(8,128)(2,1)}), bf16[8,128,256]{1,2,0:T(8,128)(2,1)S(1)}, u32[]{:S(2)}, u32[]{:S(2)}) %all-to-all-start.4) | async-done | bytes 524320 | tf_op jit(solution)/shard_map/all_to_all | solution.py:117
  148.3 0.8 copy-done.2
  149.1 3.6 %all-to-all-start.7 = ((bf16[4,128,2048]{2,1,0:T(8,128)(2,1)}), bf16[4,128,2048]{2,1,0:T(8,128)(2,1)S(1)}, u32[]{:S(2)}, u32[]{:S(2)}) async-start(bf16[4,128,2048]{2,1,0:T(8,128)(2,1)} %reduce_sum.23), calls=%async_computation.7 | async-start | bytes 4194304 | tf_op jit(solution)/shard_map/all_to_all | solution.py:63
  152.8 43.0 %reduce-scatter.2.cloned.1.call-done = f32[512,2,512]{0,2,1:T(8,128)} async-done(((f32[2048,2,512]{0,2,1:T(8,128)}), f32[512,2,512]{0,2,1:T(8,128)}) %reduce-scatter.2.cloned.1.call-update) | async-done | bytes 2097168 | tf_op jit(solution)/shard_map/reduce_scatter | solution.py:71
  195.8 4.1 %copy.103 = f32[512,2,512]{2,1,0:T(2,128)} copy(f32[512,2,512]{0,2,1:T(8,128)} %reduce-scatter.2.cloned.1.call-done) | data formatting | bytes 4194304 | tf_op jit(solution)/shard_map/reduce_scatter | solution.py:71
  199.9 0.6 dynamic-slice
  201.2 1.1 convert_element_type.91
  202.3 1.4 copy.98
  203.7 2.3 add_convert_fusion.1
  206.0 0.4 convert_reduce_fusion
  206.4 0.9 fusion.11
  207.4 75.6 %all-reduce.7.cloned.1.call-done = f32[512,2,512]{2,1,0:T(2,128)} async-done(((f32[512,2,512]{2,1,0:T(2,128)}), f32[512,2,512]{2,1,0:T(2,128)}) %all-reduce.7.cloned.1.call-update) | async-done | bytes 2097168
  283.0 1.2 constant_dynamic-slice_fusion.1
  284.2 1.0 subtract_convert_fusion
  (50 shorter events, 0.3 us)
Async XLA Ops:
  7.2 22.4 %copy-start.3 = (bf16[1,128,2048]{2,1,0:T(8,128)(2,1)S(1)}, bf16[1,128,2048]{2,1,0:T(8,128)(2,1)}, u32[]{:S(2)}) copy-start(bf16[1,128,2048]{2,1,0:T(8,128)(2,1)} %param.19) | copy-start | bytes 1572868
  7.2 87.5 %all-gather.2.cloned.1.call-start = ((), (), s32[]{:S(2)}) async-start(), calls=%async_computation.9 | async-start | bytes 4325376 | tf_op jit(solution)/shard_map/all_gather | solution.py:44
  25.3 30.5 %all-to-all-start = ((bf16[4,1,128,2048]{3,2,1,0:T(8,128)(2,1)}), bf16[4,1,128,2048]{3,2,1,0:T(8,128)(2,1)S(1)}, u32[]{:S(2)}, u32[]{:S(2)}) async-start(bf16[4,1,128,2048]{3,2,1,0:T(8,128)(2,1)} %broadcast_in_dim.57), calls=%async_computation | async-start | bytes 4194304 | tf_op jit(solution)/shard_map/all_to_all | solution.py:20
  64.6 39.1 %all-to-all-start.5 = ((bf16[128,8,256]{0,2,1:T(8,128)(2,1)}), bf16[128,8,256]{0,2,1:T(8,128)(2,1)S(1)}, u32[]{:S(2)}, u32[]{:S(2)}) async-start(bf16[128,8,256]{0,2,1:T(8,128)(2,1)} %bitcast.17), calls=%async_computation.5 | async-start | bytes 1048576 | tf_op jit(solution)/shard_map/all_to_all | solution.py:121
  68.1 127.7 %reduce-scatter.2.cloned.1.call-start = ((), (), s32[]{:S(2)}) async-start(), calls=%async_computation.10 | async-start | bytes 10485760 | tf_op jit(solution)/shard_map/reduce_scatter | solution.py:71
  94.7 3.4 %copy-start = (bf16[2,4,1,128,2048]{4,3,0,1,2:T(8,128)(2,1)S(1)}, bf16[2,4,1,128,2048]{4,3,0,1,2:T(8,128)(2,1)}, u32[]{:S(2)}) copy-start(bf16[2,4,1,128,2048]{4,3,0,1,2:T(8,128)(2,1)} %copy.94) | copy-start | bytes 12582916
  97.3 4.0 %copy-start.9 = (bf16[2048,256]{1,0:T(8,128)(2,1)}, bf16[2048,256]{1,0:T(8,128)(2,1)S(1)}, u32[]{:S(2)}) copy-start(bf16[2048,256]{1,0:T(8,128)(2,1)S(1)} %get-tuple-element.47) | copy-start | bytes 3145732
  97.3 4.0 %copy-start.11 = (bf16[2048,256]{1,0:T(8,128)(2,1)}, bf16[2048,256]{1,0:T(8,128)(2,1)S(1)}, u32[]{:S(2)}) copy-start(bf16[2048,256]{1,0:T(8,128)(2,1)S(1)} %get-tuple-element.48) | copy-start | bytes 3145732
  97.3 4.0 %copy-start.13 = (bf16[2048,256]{1,0:T(8,128)(2,1)}, bf16[2048,256]{1,0:T(8,128)(2,1)S(1)}, u32[]{:S(2)}) copy-start(bf16[2048,256]{1,0:T(8,128)(2,1)S(1)} %get-tuple-element.46) | copy-start | bytes 3145732
  97.3 4.0 %copy-start.15 = (bf16[2048,256]{1,0:T(8,128)(2,1)}, bf16[2048,256]{1,0:T(8,128)(2,1)S(1)}, u32[]{:S(2)}) copy-start(bf16[2048,256]{1,0:T(8,128)(2,1)S(1)} %get-tuple-element.49) | copy-start | bytes 3145732
  103.7 2.6 copy-start.1
  104.4 4.6 %copy-start.5 = (bf16[1024,256]{0,1:T(8,128)(2,1)}, bf16[1024,256]{0,1:T(8,128)(2,1)S(1)}, u32[]{:S(2)}) copy-start(bf16[1024,256]{0,1:T(8,128)(2,1)S(1)} %get-tuple-element.50) | copy-start | bytes 1572868
  104.4 4.6 %copy-start.7 = (bf16[1024,256]{0,1:T(8,128)(2,1)}, bf16[1024,256]{0,1:T(8,128)(2,1)S(1)}, u32[]{:S(2)}) copy-start(bf16[1024,256]{0,1:T(8,128)(2,1)S(1)} %get-tuple-element.51) | copy-start | bytes 1572868
  115.2 1.1 copy-start.6
  115.2 1.4 copy-start.8
  115.2 1.7 copy-start.14
  117.0 4.0 %copy-start.10 = (bf16[2048,256]{1,0:T(8,128)(2,1)S(1)}, bf16[2048,256]{1,0:T(8,128)(2,1)}, u32[]{:S(2)}) copy-start(bf16[2048,256]{1,0:T(8,128)(2,1)} %copy-done.9) | copy-start | bytes 3145732
  117.0 4.0 %copy-start.12 = (bf16[2048,256]{1,0:T(8,128)(2,1)S(1)}, bf16[2048,256]{1,0:T(8,128)(2,1)}, u32[]{:S(2)}) copy-start(bf16[2048,256]{1,0:T(8,128)(2,1)} %copy-done.11) | copy-start | bytes 3145732
  133.7 14.6 %all-to-all-start.4 = ((bf16[8,128,256]{1,2,0:T(8,128)(2,1)}), bf16[8,128,256]{1,2,0:T(8,128)(2,1)S(1)}, u32[]{:S(2)}, u32[]{:S(2)}) async-start(bf16[8,128,256]{1,2,0:T(8,128)(2,1)} %bitcast.74), calls=%async_computation.4 | async-start | bytes 1048576 | tf_op jit(solution)/shard_map/all_to_all | solution.py:117
  148.3 0.8 copy-start.2
  149.1 57.0 %all-to-all-start.7 = ((bf16[4,128,2048]{2,1,0:T(8,128)(2,1)}), bf16[4,128,2048]{2,1,0:T(8,128)(2,1)S(1)}, u32[]{:S(2)}, u32[]{:S(2)}) async-start(bf16[4,128,2048]{2,1,0:T(8,128)(2,1)} %reduce_sum.23), calls=%async_computation.7 | async-start | bytes 4194304 | tf_op jit(solution)/shard_map/all_to_all | solution.py:63
  152.7 47.2 %copy-start.22 = (u32[256]{0:T(256)S(1)}, u32[256]{0:T(256)}, u32[]{:S(2)}) copy-start(u32[256]{0:T(256)} %constant.60) | copy-start | bytes 3076
  152.7 130.3 %all-reduce.7.cloned.1.call-start = ((), (), s32[]{:S(2)}) async-start(), calls=%async_computation.11 | async-start | bytes 4194304
  203.6 2.8 copy-start.4
  203.6 80.5 %copy-start.16 = (bf16[2,64,256]{2,1,0:T(8,128)(2,1)S(1)}, bf16[2,64,256]{2,1,0:T(8,128)(2,1)}, u32[]{:S(2)}) copy-start(bf16[2,64,256]{2,1,0:T(8,128)(2,1)} %param.14) | copy-start | bytes 196612
  203.6 80.5 %copy-start.17 = (bf16[2,64,256]{2,1,0:T(8,128)(2,1)S(1)}, bf16[2,64,256]{2,1,0:T(8,128)(2,1)}, u32[]{:S(2)}) copy-start(bf16[2,64,256]{2,1,0:T(8,128)(2,1)} %param.13) | copy-start | bytes 196612
  203.7 80.5 %copy-start.18 = (f32[2,64,256]{2,1,0:T(8,128)S(1)}, f32[2,64,256]{2,1,0:T(8,128)}, u32[]{:S(2)}) copy-start(f32[2,64,256]{2,1,0:T(8,128)} %param.17) | copy-start | bytes 393220
  203.7 80.5 %copy-start.19 = (f32[2,64,256]{2,1,0:T(8,128)S(1)}, f32[2,64,256]{2,1,0:T(8,128)}, u32[]{:S(2)}) copy-start(f32[2,64,256]{2,1,0:T(8,128)} %param.18) | copy-start | bytes 393220
  203.7 80.5 %copy-start.20 = (f32[2,64,256]{2,1,0:T(8,128)S(1)}, f32[2,64,256]{2,1,0:T(8,128)}, u32[]{:S(2)}) copy-start(f32[2,64,256]{2,1,0:T(8,128)} %param.16) | copy-start | bytes 393220
  203.7 80.5 %copy-start.21 = (f32[2,64,256]{2,1,0:T(8,128)S(1)}, f32[2,64,256]{2,1,0:T(8,128)}, u32[]{:S(2)}) copy-start(f32[2,64,256]{2,1,0:T(8,128)} %param.15) | copy-start | bytes 393220
Sparse Core Ops, SparseCore 0:
  11.2 83.4 all-gather.1
  115.4 80.3 reduce-scatter.1
  200.0 82.9 all-reduce.6
where the time goes:
time: 293 us; the launch traced here: 292 us
  waiting for transfers between devices  171 us (58%)
  blocking collectives  29.5 us (10%)
  local copies, waits for them, and re-layouts  24.9 us (8%)
  matrix products  18.7 us (6%)
  other arithmetic  17.1 us (6%)
  between operations  15.4 us (5%)
  starting transfers between devices  15.1 us (5%)
    unnamed x4, waiting for transfers between devices  75.7 us
    reduce_scatter x1, waiting for transfers between devices, sum_by_axis(): so_far = lax.psum_scatter(so_far, axis, scatter_dimension=0, tiled=True)  43 us
    all_to_all x1, waiting for transfers between devices, copy_for_each(): lax.all_to_all(jnp.broadcast_to(array[None], (length, *array.shape)), axi...  25.2 us
    all_gather x1, waiting for transfers between devices, sent_together(): lax.all_gather(both, axis, axis=dim, tiled=True)  21.7 us
    all_to_all x3, blocking collectives, copy_for_each(): lax.all_to_all(jnp.broadcast_to(array[None], (length, *array.shape)), axi...  21.4 us
    all_to_all x1, blocking collectives, sum_at_owner(): lax.all_to_all(split_up(array, dim, length), axis, 0, 0, tiled=True)  8.18 us
  transfers between devices with their start and end apart: 7, of which 5 were waited for; matrix products, arithmetic and copies ran while one was open for 15% of the time, Pallas kernels for 0%

commit v1 on v0

v1 whole, which is shorter than its diff:
```python
import jax
import jax.numpy as jnp
from jax import lax
from jax.experimental import pallas as pl
from jax.experimental.pallas import tpu as pltpu
from jax.sharding import Mesh
from jax.sharding import PartitionSpec as P

STEP = 10
BETA_ONE = 0.9
BETA_TWO = 0.95
LEARN_RATE = 0.001
EPSILON = 1e-08

NX, NZ, NY, NC = 4, 8, 4, 2
ROWS = 128
LEN = 1024
CH = 2048
COLS = 256
KB = 64
PAD = 256
CA = 512
CB = 4 * COLS - CA
F32 = jnp.float32
BF16 = jnp.bfloat16
NSEM = 320
MESH = pl.DeviceIdType.MESH


def turn(position, by, size):
    return lax.rem(position + (by + size), size)


def kernel(
    dil_ref, x_in, ids_in, fw_in, gw_in, cot_in,
    lay_out, dx_out, grad_out,
    xb, xt, wb, u0, u1, dl, dd, cotc, gcol, grow, cotv, idc, idr, idsrc,
    dw, ra, za, rb, rbx, dxb, sib, yr, ssem, rsem, lsem,
):
    x, z = lax.axis_index("x"), lax.axis_index("z")
    y, c = lax.axis_index("y"), lax.axis_index("c")
    me = y * 2 + c
    d = dil_ref[0]

    def at_x(k):
        return turn(x, k, NX)

    def at_z(k):
        return turn(z, k, NZ)

    def at_y(k):
        return turn(y, k, NY)

    oc = 1 - c
    number = {}
    sent = []

    def slot(key):
        return number.setdefault(key, len(number))

    def send(key, src, dst, dev):
        i = slot(key)
        copy = pltpu.make_async_remote_copy(
            src_ref=src, dst_ref=dst, send_sem=ssem.at[i], recv_sem=rsem.at[i],
            device_id=dev, device_id_type=MESH,
        )
        copy.start()
        sent.append(copy)

    def arrived(key, dst, dev):
        i = slot(key)
        pltpu.make_async_remote_copy(
            src_ref=dst, dst_ref=dst, send_sem=ssem.at[i], recv_sem=rsem.at[i],
            device_id=dev, device_id_type=MESH,
        ).wait_recv()

    local = []

    def bring(src, dst):
        copy = pltpu.make_async_copy(src, dst, lsem.at[len(local)])
        copy.start()
        local.append(copy)

    def rows_of(ref, block):
        return ref.at[pl.ds(pl.multiple_of(block * ROWS, ROWS), ROWS)]

    def cols_of(ref, block):
        return ref.at[:, pl.ds(pl.multiple_of(block * COLS, COLS), COLS)]

    for tap in range(2):
        bring(fw_in.at[tap], wb.at[x, z, :, pl.ds(tap * 512, COLS)])
        bring(gw_in.at[tap], wb.at[x, z, :, pl.ds(tap * 512 + COLS, COLS)])
    bring(x_in, rows_of(xb, me))
    bring(cot_in, cotv)
    idsrc[...] = jnp.broadcast_to(ids_in[...], (8, ROWS))

    barrier = pltpu.get_barrier_semaphore()
    ctx_peers = [
        {"y": at_y(k), "c": cc} for k in range(4) for cc in (c, oc) if (k, cc is c) != (0, True)
    ]
    peers = ctx_peers + [{"x": at_x(k)} for k in (1, 2, 3)] + [{"z": at_z(k)} for k in (1, -1)]
    for dev in peers:
        pl.semaphore_signal(barrier, inc=1, device_id=dev, device_id_type=MESH)
    pl.semaphore_wait(barrier, len(peers))
    for copy in local:
        copy.wait()

    def wa(xi, zi, lo=0, n=KB):
        return wb.at[xi, zi, pl.ds(lo, n), pl.ds(0, CA)]

    def wbp(xi, zi):
        return wb.at[xi, zi, :, pl.ds(CA, CB)]

    def half(block, h, ref=None):
        ref = xb if ref is None else ref
        return ref.at[pl.ds(pl.multiple_of(block * ROWS + h * 64, 64), 64)]

    ups = {"z": at_z(1)}
    downs = {"z": at_z(-1)}

    def z_send_a(r):
        if r < 3:
            send(("za", 1, r), wa(x, at_z(-r)), wa(x, at_z(-r)), ups)
            send(("za", -1, r), wa(x, at_z(r)), wa(x, at_z(r)), downs)
        else:
            send(("za", 1, r), wa(x, at_z(-r), 0, 32), wa(x, at_z(-r), 0, 32), ups)
            send(("za", -1, r), wa(x, at_z(r), 32, 32), wa(x, at_z(r), 32, 32), downs)

    def z_got_a(r):
        if r < 4:
            arrived(("za", 1, r - 1), wa(x, at_z(-r)), downs)
            arrived(("za", -1, r - 1), wa(x, at_z(r)), ups)
        else:
            arrived(("za", 1, r - 1), wa(x, at_z(-r), 0, 32), downs)
            arrived(("za", -1, r - 1), wa(x, at_z(r), 32, 32), ups)

    def x_send_a(r):
        for k in (1, 2, 3):
            send(("xa", r, k), wa(x, at_z(r)), wa(x, at_z(r)), {"x": at_x(k)})

    def x_got_a(r):
        for k in (1, 2, 3):
            arrived(("xa", r, k), wa(at_x(-k), at_z(r)), {"x": at_x(-k)})

    def carried(direction, r):
        return (0, 1, 2, 3) if r < 4 else ((0, 1) if direction > 0 else (2, 3))

    def z_send_b(r, k):
        for s, dev in ((1, ups), (-1, downs)):
            if k in carried(s, r + 1):
                ref = wbp(at_x(k), at_z(-s * r))
                send(("zb", s, r, k), ref, ref, dev)

    def z_got_b(r, k):
        for s, dev in ((1, downs), (-1, ups)):
            if k in carried(s, r):
                arrived(("zb", s, r - 1, k), wbp(at_x(k), at_z(-s * r)), dev)

    z_send_a(0)
    for k in (1, 2, 3):
        send(("xb", k), wbp(x, z), wbp(x, z), {"x": at_x(k)})
    for s, h in ((1, 0), (-1, 1)):
        send(("X", s, 0), half(me, h), half(me, h), {"y": at_y(s)})
    send(("Xc", 0), rows_of(xb, me), rows_of(xb, me), {"c": oc})
    z_send_b(0, 0)
    x_send_a(0)
    for s, h in ((1, 1), (-1, 0)):
        send(("X", s, 1), half(me, h), half(me, h), {"y": at_y(s)})
    ctx_offsets = [(k, o) for k in range(4) for o in (0, 1) if (k, o) != (0, 0)]

    def ctx_dev(k, o):
        return {"y": at_y(k), "c": turn(c, o, NC)}

    def ctx_id(k, o):
        return at_y(k) * 2 + turn(c, o, NC)

    for k, o in ctx_offsets:
        send(("id", k, o), idsrc, idr.at[me], ctx_dev(k, o))

    idr[me] = idsrc[...]
    idc[pl.ds(0, PAD)] = jnp.full((PAD, 128), -1, jnp.int32)
    idc[pl.ds(PAD + LEN, PAD)] = jnp.full((PAD, 128), -2, jnp.int32)
    u1[:, pl.ds(0, PAD)] = jnp.zeros((4, PAD, 128), F32)
    dl[:, pl.ds(LEN, PAD)] = jnp.zeros((4, PAD, 128), F32)

    def transposed(block):
        rows = pl.ds(pl.multiple_of(block * ROWS, ROWS), ROWS)

        @pl.loop(0, NX)
        def _(xi):
            part = xb[rows, pl.ds(pl.multiple_of(xi * 512, 512), 512)]
            xt[xi, :, :, rows] = part.T.reshape(NZ, KB, ROWS)

    z_got_a(1)
    z_send_a(1)
    for r in (1, -1):
        x_send_a(r)
    for k in (1, 2, 3):
        arrived(("xb", k), wbp(at_x(-k), z), {"x": at_x(-k)})
        z_send_b(0, 4 - k)
    z_got_b(1, 0)
    z_send_b(1, 0)
    transposed(me)
    arrived(("X", 1, 0), half(at_y(-1) * 2 + c, 0), {"y": at_y(-1)})
    send(("X", 1, 2), half(at_y(-1) * 2 + c, 0), half(at_y(-1) * 2 + c, 0), {"y": at_y(1)})
    arrived(("X", -1, 0), half(at_y(1) * 2 + c, 1), {"y": at_y(1)})
    send(("X", -1, 2), half(at_y(1) * 2 + c, 1), half(at_y(1) * 2 + c, 1), {"y": at_y(-1)})
    z_got_a(2)
    z_send_a(2)
    for r in (2, -2):
        x_send_a(r)
    for k, o in ctx_offsets:
        send(("cot", k, o), cols_of(cotv, ctx_id(k, o)), rows_of(cotc, me), ctx_dev(k, o))
    for part in range(2):
        rows = pl.ds(pl.multiple_of(me * ROWS + part * 64, 64), 64)
        cotc[rows] = cotv[pl.ds(part * 64, 64), pl.ds(pl.multiple_of(me * COLS, COLS), COLS)]
    arrived(("Xc", 0), rows_of(xb, y * 2 + oc), {"c": oc})
    transposed(y * 2 + oc)
    for k in (3, 2, 1):
        z_got_b(1, k)
        z_send_b(1, k)
    arrived(("X", 1, 1), half(at_y(-1) * 2 + c, 1), {"y": at_y(-1)})
    send(("Xc", 1), rows_of(xb, at_y(-1) * 2 + c), rows_of(xb, at_y(-1) * 2 + c), {"c": oc})
    arrived(("X", -1, 1), half(at_y(1) * 2 + c, 0), {"y": at_y(1)})
    send(("Xc", 2), rows_of(xb, at_y(1) * 2 + c), rows_of(xb, at_y(1) * 2 + c), {"c": oc})
    z_got_a(3)
    z_send_a(3)
    for r in (3, -3):
        x_send_a(r)
    z_got_b(2, 0)
    z_send_b(2, 0)
    transposed(at_y(-1) * 2 + c)
    z_got_b(2, 3)
    z_send_b(2, 3)
    transposed(at_y(1) * 2 + c)
    for k in (2, 1):
        z_got_b(2, k)
        z_send_b(2, k)
    z_got_a(4)
    x_send_a(4)
    arrived(("Xc", 1), rows_of(xb, at_y(-1) * 2 + oc), {"c": oc})
    transposed(at_y(-1) * 2 + oc)
    arrived(("Xc", 2), rows_of(xb, at_y(1) * 2 + oc), {"c": oc})
    transposed(at_y(1) * 2 + oc)
    z_got_b(3, 0)
    z_send_b(3, 0)
    z_got_b(3, 3)
    z_send_b(3, 3)
    arrived(("X", 1, 2), half(at_y(2) * 2 + c, 0), {"y": at_y(-1)})
    arrived(("X", -1, 2), half(at_y(2) * 2 + c, 1), {"y": at_y(1)})
    send(("Xc", 3), rows_of(xb, at_y(2) * 2 + c), rows_of(xb, at_y(2) * 2 + c), {"c": oc})
    for k in (2, 1):
        z_got_b(3, k)
        z_send_b(3, k)
    transposed(at_y(2) * 2 + c)
    for k, o in ctx_offsets:
        arrived(("id", k, o), idr.at[ctx_id(-k, o)], ctx_dev(-k, o))

    @pl.loop(0, NY * NC)
    def _(block):
        spread = jnp.broadcast_to(idr[block, 0:1, :], (ROWS, ROWS))
        idc[pl.ds(pl.multiple_of(PAD + block * ROWS, ROWS), ROWS)] = spread.T

    arrived(("Xc", 3), rows_of(xb, at_y(2) * 2 + oc), {"c": oc})
    transposed(at_y(2) * 2 + oc)

    def forward(pair, first):
        @pl.loop(0, 4)
        def _(i):
            rows = pl.ds(pl.multiple_of(i * 256, 256), 256)
            lags = pl.ds(pl.multiple_of(PAD + i * 256, 256), 256)
            lhs = jnp.concatenate(
                [
                    xb[rows, pl.ds(pl.multiple_of(xi * 512 + pair * 128, 128), 128)]
                    for xi in range(NX)
                ],
                axis=1,
            )
            w0 = wb[:, pl.ds(pair * 2, 2), :, pl.ds(0, 512)].reshape(512, 512)
            w1 = wb[:, pl.ds(pair * 2, 2), :, pl.ds(512, 512)].reshape(512, 512)
            p0 = jnp.dot(lhs, w0, preferred_element_type=F32)
            p1 = jnp.dot(lhs, w1, preferred_element_type=F32)
            u0[rows] = p0 if first else u0[rows] + p0
            for j in range(4):
                part = p1[:, j * 128 : j * 128 + 128]
                u1[j, lags] = part if first else u1[j, lags] + part

    pair = z // 2
    lean = 1 - 2 * lax.rem(z, 2)
    for r in (0, 1, -1):
        x_got_a(r)
    forward(pair, True)
    for r in (2, -2):
        x_got_a(r)
    forward(turn(pair, -lean, 4), False)
    for r in (3, -3):
        x_got_a(r)
    forward(turn(pair, lean, 4), False)
    x_got_a(4)
    for k in range(4):
        z_got_b(4, k)
    forward(turn(pair, 2, 4), False)
    for k, o in ctx_offsets:
        arrived(("cot", k, o), rows_of(cotc, ctx_id(-k, o)), ctx_dev(-k, o))

    @pl.loop(0, LEN // 128)
    def _(i):
        t0 = pl.multiple_of(i * 128, 128)
        same = idc[pl.ds(PAD + t0, 128)] == idc[pl.ds(PAD + t0 - d, 128)]
        for j in range(2):
            pre = []
            for part in range(2):
                cols = pl.ds(part * COLS + j * 128, 128)
                lag = u1[part * 2 + j, pl.ds(PAD + t0 - d, 128)]
                pre.append(u0[pl.ds(t0, 128), cols] + jnp.where(same, lag, 0.0))
            f = jnp.tanh(pre[0])
            g = jax.nn.sigmoid(pre[1])
            near = pl.ds(j * 128, 128)
            far = pl.ds(COLS + j * 128, 128)
            gcol[pl.ds(t0, 128), near] = (f * g).astype(BF16)
            cot = cotc[pl.ds(t0, 128), near].astype(F32)
            fd = (cot * g * (1.0 - f * f)).astype(BF16)
            gd = (cot * f * g * (1.0 - g)).astype(BF16)
            dd[pl.ds(t0, 128), near] = fd
            dd[pl.ds(t0, 128), far] = gd
            dl[j, pl.ds(t0, 128)] = fd.astype(F32)
            dl[2 + j, pl.ds(t0, 128)] = gd.astype(F32)

    for k, o in ctx_offsets:
        send(("gat", k, o), rows_of(gcol, ctx_id(k, o)), cols_of(grow, me), ctx_dev(k, o))
    for part in range(2):
        rows = pl.ds(pl.multiple_of(me * ROWS + part * 64, 64), 64)
        grow[pl.ds(part * 64, 64), pl.ds(pl.multiple_of(me * COLS, COLS), COLS)] = gcol[rows]

    @pl.loop(0, LEN // 128)
    def _(i):
        t0 = pl.multiple_of(i * 128, 128)
        same = idc[pl.ds(PAD + t0, 128)] == idc[pl.ds(PAD + t0 + d, 128)]
        for j in range(4):
            ahead = dl[j, pl.ds(t0 + d, 128)]
            dd[pl.ds(t0, 128), pl.ds(512 + j * 128, 128)] = jnp.where(same, ahead, 0.0).astype(BF16)

    def grad_w(r):
        zi = at_z(r)
        for part in range(2):
            lhs = xt[:, zi].reshape(NX * KB, LEN)
            out = jnp.dot(lhs, dd[:, pl.ds(part * 512, 512)], preferred_element_type=F32)
            dw[:, zi, :, pl.ds(part * 512, 512)] = out.astype(BF16).reshape(NX, KB, 512)

    def da(xi, zi, lo=0, n=KB):
        return dw.at[xi, zi, pl.ds(lo, n), pl.ds(0, CA)]

    def db(xi, zi):
        return dw.at[xi, zi, :, pl.ds(CA, CB)]

    def sum_x_send(r):
        for k in (1, 2, 3):
            send(("sxa", r, k), da(at_x(k), at_z(r)), ra.at[k - 1, at_z(r)], {"x": at_x(k)})

    def sum_x_got(r):
        for k in (1, 2, 3):
            arrived(("sxa", r, k), ra.at[k - 1, at_z(r)], {"x": at_x(-k)})

    def a_sum(r):
        zi = at_z(r)
        return (da(x, zi)[...].astype(F32) + ra[0, zi].astype(F32)) + (
            ra[1, zi].astype(F32) + ra[2, zi].astype(F32)
        )

    def a_far():
        sum_x_got(4)
        da(x, at_z(4))[...] = a_sum(4).astype(BF16)
        send(("sza", 1, 4), da(x, at_z(4), 0, 32), za.at[0, 3, pl.ds(0, 32)], ups)
        send(("sza", -1, 4), da(x, at_z(-4), 32, 32), za.at[1, 3, pl.ds(32, 32)], downs)

    def a_step(r):
        for s, h, dev, src in ((1, 0, ups, downs), (-1, 1, downs, ups)):
            sum_x_got(s * r)
            total = a_sum(s * r)
            ref = da(x, at_z(s * r))
            if r == 3:
                lo = pl.ds(h * 32, 32)
                arrived(("sza", s, r + 1), za.at[h, r, lo], src)
                ref[...] = total.astype(BF16)
                part = total[h * 32 : h * 32 + 32] + za[h, r, lo].astype(F32)
                da(x, at_z(s * r), h * 32, 32)[...] = part.astype(BF16)
            else:
                arrived(("sza", s, r + 1), za.at[h, r], src)
                ref[...] = (total + za[h, r].astype(F32)).astype(BF16)
            send(("sza", s, r), ref, za.at[h, r - 1], dev)

    def b_far():
        for s, h, dev in ((1, 0, ups), (-1, 1, downs)):
            for k in carried(s, 4):
                send(("szb", s, 4, k), db(at_x(k), at_z(s * 4)), rb.at[h, 3, k], dev)

    def b_step(r, k):
        for s, h, dev, src in ((1, 0, ups, downs), (-1, 1, downs, ups)):
            ref = db(at_x(k), at_z(s * r))
            if k in carried(s, r + 1):
                arrived(("szb", s, r + 1, k), rb.at[h, r, k], src)
                ref[...] = (ref[...].astype(F32) + rb[h, r, k].astype(F32)).astype(BF16)
            send(("szb", s, r, k), ref, rb.at[h, r - 1, k], dev)

    def b_last(k):
        for s, h, src in ((1, 0, downs), (-1, 1, ups)):
            arrived(("szb", s, 1, k), rb.at[h, 0, k], src)
        ref = db(at_x(k), z)
        total = ref[...].astype(F32) + (rb[0, 0, k].astype(F32) + rb[1, 0, k].astype(F32))
        if k == 0:
            grad_out[:, pl.ds(CA, CB)] = total
        else:
            ref[...] = total.astype(BF16)
            send(("sxb", k), ref, rbx.at[k - 1], {"x": at_x(k)})

    def grad_x(k):
        yi = at_y(k)
        lhs = dd[pl.ds(pl.multiple_of(yi * 256, 256), 256), :]

        @pl.loop(0, NX)
        def _(xi):
            out = lax.dot_general(
                lhs, wb[xi].reshape(512, 1024), (((1,), (1,)), ((), ())), preferred_element_type=F32
            )
            out = out.astype(BF16).reshape(NC, ROWS, 512)
            dxb[yi, :, :, pl.ds(pl.multiple_of(xi * 512, 512), 512)] = out

        send(("sib", k), dxb.at[yi, oc], sib.at[yi], {"c": oc})

    def pair_sum(k):
        yi = at_y(k)
        arrived(("sib", k), sib.at[yi], {"c": oc})

        @pl.loop(0, 4)
        def _(i):
            rows = pl.ds(pl.multiple_of(i * 32, 32), 32)
            total = dxb[yi, c, rows].astype(F32) + sib[yi, rows].astype(F32)
            dxb[yi, c, rows] = total.astype(BF16)

    def y_far():
        pair_sum(2)
        for s, h in ((1, 0), (-1, 1)):
            rows = pl.ds(h * 64, 64)
            send(("y", s, 2), dxb.at[at_y(2), c, rows], yr.at[h, 0, rows], {"y": at_y(s)})

    def y_step():
        for s, h in ((1, 0), (-1, 1)):
            pair_sum(s)
            rows = pl.ds(h * 64, 64)
            yi = at_y(s)
            arrived(("y", s, 2), yr.at[h, 0, rows], {"y": at_y(-s)})

            @pl.loop(0, 2)
            def _(i):
                some = pl.ds(pl.multiple_of(h * 64 + i * 32, 32), 32)
                total = dxb[yi, c, some].astype(F32) + yr[h, 0, some].astype(F32)
                dxb[yi, c, some] = total.astype(BF16)

            send(("y", s, 1), dxb.at[yi, c], yr.at[h, 1], {"y": at_y(s)})

    grad_w(4)
    sum_x_send(4)
    b_far()
    grad_x(2)
    grad_w(3)
    sum_x_send(3)
    grad_w(-3)
    sum_x_send(-3)
    y_far()
    for k in range(4):
        b_step(3, k)
    a_far()
    grad_x(1)
    grad_w(2)
    sum_x_send(2)
    grad_w(-2)
    sum_x_send(-2)
    grad_x(-1)
    for k in range(4):
        b_step(2, k)
    a_step(3)
    y_step()
    grad_w(1)
    sum_x_send(1)
    grad_w(-1)
    sum_x_send(-1)
    grad_w(0)
    sum_x_send(0)
    a_step(2)
    grad_x(0)
    for k in range(4):
        b_step(1, k)
    for k, o in ctx_offsets:
        arrived(("gat", k, o), cols_of(grow, ctx_id(-k, o)), ctx_dev(-k, o))

    @pl.loop(0, 4)
    def _(i):
        rows = pl.ds(pl.multiple_of(i * 32, 32), 32)
        mine = xb[pl.ds(pl.multiple_of(me * ROWS + i * 32, 32), 32)]
        lay_out[rows] = (mine.astype(F32) + grow[rows].astype(F32)).astype(BF16)

    pair_sum(0)
    a_step(1)
    for k in (1, 2, 3, 0):
        b_last(k)
    for s, h in ((1, 0), (-1, 1)):
        arrived(("y", s, 1), yr.at[h, 1], {"y": at_y(-s)})

    @pl.loop(0, 4)
    def _(i):
        rows = pl.ds(pl.multiple_of(i * 32, 32), 32)
        back = dxb[y, c, rows].astype(F32) + (yr[0, 1, rows].astype(F32) + yr[1, 1, rows].astype(F32))
        dx_out[rows] = (cotv[rows].astype(F32) + back).astype(BF16)

    sum_x_got(0)
    total = a_sum(0)
    for s, h, src in ((1, 0, downs), (-1, 1, ups)):
        arrived(("sza", s, 1), za.at[h, 0], src)
    grad_out[:, pl.ds(0, CA)] = total + (za[0, 0].astype(F32) + za[1, 0].astype(F32))
    for k in (1, 2, 3):
        arrived(("sxb", k), rbx.at[k - 1], {"x": at_x(-k)})
    grad_out[:, pl.ds(CA, CB)] += rbx[0].astype(F32) + rbx[1].astype(F32) + rbx[2].astype(F32)
    for copy in sent:
        copy.wait_send()


def fused(dilation, inputs, ids, fw, gw, cot):
    any_space = pl.BlockSpec(memory_space=pl.ANY)
    vmem = pl.BlockSpec(memory_space=pltpu.VMEM)
    scratch = [
        ((LEN, CH), BF16),
        ((NX, NZ, KB, LEN), BF16),
        ((NX, NZ, KB, 4 * COLS), BF16),
        ((LEN, 2 * COLS), F32),
        ((4, PAD + LEN, 128), F32),
        ((4, LEN + PAD, 128), F32),
        ((LEN, 4 * COLS), BF16),
        ((LEN, COLS), BF16),
        ((LEN, COLS), BF16),
        ((ROWS, CH), BF16),
        ((ROWS, CH), BF16),
        ((PAD + LEN + PAD, 128), jnp.int32),
        ((NY * NC, 8, ROWS), jnp.int32),
        ((8, ROWS), jnp.int32),
        ((NX, NZ, KB, 4 * COLS), BF16),
        ((3, NZ, KB, CA), BF16),
        ((2, 4, KB, CA), BF16),
        ((2, 4, NX, KB, CB), BF16),
        ((3, KB, CB), BF16),
        ((NY, NC, ROWS, CH), BF16),
        ((NY, ROWS, CH), BF16),
        ((2, 2, ROWS, CH), BF16),
    ]
    return pl.pallas_call(
        kernel,
        name="layer",
        out_shape=(
            jax.ShapeDtypeStruct((ROWS, CH), BF16),
            jax.ShapeDtypeStruct((ROWS, CH), BF16),
            jax.ShapeDtypeStruct((KB, 4 * COLS), F32),
        ),
        in_specs=[
            pl.BlockSpec(memory_space=pltpu.SMEM), any_space, vmem, any_space, any_space, any_space,
        ],
        out_specs=(vmem, vmem, vmem),
        scratch_shapes=[pltpu.VMEM(s, t) for s, t in scratch]
        + [
            pltpu.SemaphoreType.DMA((NSEM,)),
            pltpu.SemaphoreType.DMA((NSEM,)),
            pltpu.SemaphoreType.DMA((6,)),
        ],
        compiler_params=pltpu.CompilerParams(
            collective_id=0, has_side_effects=True, vmem_limit_bytes=60 * 2**20
        ),
        cost_estimate=pl.CostEstimate(flops=13 * 10**9, bytes_accessed=2**23, transcendentals=2**20),
    )(dilation, inputs, ids, fw, gw, cot)


def adam_update(weight, moment, second, gradient):
    new_moment = BETA_ONE * moment + (1.0 - BETA_ONE) * gradient
    new_second = BETA_TWO * second + (1.0 - BETA_TWO) * gradient * gradient
    first_fix = 1.0 - BETA_ONE**STEP
    second_fix = 1.0 - BETA_TWO**STEP
    step_size = new_moment / first_fix / (jnp.sqrt(new_second / second_fix) + EPSILON)
    new_weight = (weight.astype(F32) - LEARN_RATE * step_size).astype(BF16)
    return (new_weight, new_moment, new_second)


def per_device(inputs, doc_ids, dilation, fw, gw, fm, fv, gm, gv, cotangent):
    layer_out, input_grad, grads = fused(dilation, inputs[0], doc_ids, fw, gw, cotangent[0])
    grads = grads / (LEN * NX * NZ)
    filter_grad = jnp.stack([grads[:, 0:256], grads[:, 512:768]])
    gate_grad = jnp.stack([grads[:, 256:512], grads[:, 768:1024]])
    new_fw, new_fm, new_fv = adam_update(fw, fm, fv, filter_grad)
    new_gw, new_gm, new_gv = adam_update(gw, gm, gv, gate_grad)
    return (layer_out[None], input_grad[None], new_fw, new_gw, new_fm, new_fv, new_gm, new_gv)


def solution(mesh):
    torus = Mesh(mesh.devices.reshape(NX, NZ, NY, NC), ("x", "z", "y", "c"))
    dp, ctx = ("x", "z"), ("y", "c")
    rows, weights = P(dp, ctx, None), P(None, dp, ctx)
    return jax.shard_map(
        per_device,
        mesh=torus,
        in_specs=(rows, P(dp, ctx), P(), *[weights] * 6, rows),
        out_specs=(rows, rows, *[weights] * 6),
        check_vma=False,
    )
```

time: 293 us -> 93 us (0.32)
  waiting for transfers between devices: 171 us -> 0 us
  Pallas kernels: 0 us -> 85.3 us
  blocking collectives: 29.5 us -> 0 us
  local copies, waits for them, and re-layouts: 24.9 us -> 3.34 us
  matrix products: 18.7 us -> 0 us
  other arithmetic: 17.1 us -> 1.95 us
  starting transfers between devices: 15.1 us -> 0 us
  between operations: 15.4 us -> 1.37 us
    pallas_call x0 -> x1, Pallas kernels: none -> 85.3 us  [fused(): pl.pallas_call(kernel, name='layer', out_shape=(jax.ShapeDtypeStruct((ROW...]
    unnamed x4 -> x0, waiting for transfers between devices: 75.7 us -> none
    reduce_scatter x1 -> x0, waiting for transfers between devices: 43 us -> none  [sum_by_axis(): so_far = lax.psum_scatter(so_far, axis, scatter_dimension=0, tiled=True)]
    all_to_all x4 -> x0, waiting for transfers between devices: 30.4 us -> none  [the longest x1 25.2 us: copy_for_each(): lax.all_to_all(jnp.broadcast_to(array[None], (length, *array.shape)), axi...]
    all_to_all x4 -> x0, blocking collectives: 29.5 us -> none  [the longest x3 21.4 us: copy_for_each(): lax.all_to_all(jnp.broadcast_to(array[None], (length, *array.shape)), axi...]
    all_gather x1 -> x0, waiting for transfers between devices: 21.7 us -> none  [sent_together(): lax.all_gather(both, axis, axis=dim, tiled=True)]
    dot_general x6 -> x0, matrix products: 18.7 us -> none  [the longest x1 4.2 us: per_device(): lax.dot_general(rows_ahead, back_one, (((1,), (1,)), ((), ())), preferred...]
    all_to_all x4 -> x0, starting transfers between devices: 15 us -> none  [the longest x1 4.29 us: per_device(): lax.all_to_all(gated_cols, CTX, split_axis=0, concat_axis=1, tiled=True)]
  transfers between devices with their start and end apart: 7 -> 0, of which waited for: 5 -> 0; matrix products, arithmetic and copies ran while one was open for 15% -> 0% of each run, Pallas kernels for 0% -> 0%
where the time goes in v1:
time: 93 us; the launch traced here: 92 us
  Pallas kernels  85.3 us (92%)
  local copies, waits for them, and re-layouts  3.34 us (4%)
  other arithmetic  1.95 us (2%)
  between operations  1.37 us (1%)
    pallas_call x1, Pallas kernels, fused(): pl.pallas_call(kernel, name='layer', out_shape=(jax.ShapeDtypeStruct((ROW...  85.3 us
    unnamed x18, local copies, waits for them, and re-layouts  3.32 us

profile of v1, /device:TPU:2, one launch (start us, length us, event | category | flops | bytes accessed | tf_op | source)
XLA Modules:
  0.0 92.0 jit_solution(7358321954936969226)
XLA Ops:
  1.3 85.3 %layer.1 = (bf16[128,2048]{1,0:T(8,128)(2,1)}, bf16[128,2048]{1,0:T(8,128)(2,1)}, f32[64,1024]{1,0:T(8,128)}) custom-call(s32[1]{0:T(128)S(6)} %copy.20.dil_ref, bf16[128,2048]{1,0:T(8,128)(2,1)} %bitcast.14, s32[1,128]{1,0:T(1,128)} %ids_in.1, bf16[2,64,256]{2,1,0:T(8,128)(2,1)} %fw_in.1, bf16[2,64,256]{2,1,0:T(8,128)(2,1)} %gw_in.1, bf16[128,2048]{1,0:T(8,128)(2,1)} %bitcast.15), custom_call_target="tpu_custom_call" | custom-call | flops 12999999488 | bytes 8388608 | tf_op jit(solution)/shard_map/layer/pallas_call | solution.py:554
  86.6 0.0 copy-start.6
  86.6 0.0 copy-start.7
  86.7 1.0 %broadcast_multiply_fusion = f32[64,1024]{1,0:T(8,128)S(1)} fusion(f32[64,1024]{1,0:T(8,128)} %get-tuple-element.13), kind=kLoop, calls=%fused_computation.10 | loop fusion | flops 65536 | bytes 524288 | tf_op jit(solution)/shard_map/div | solution.py:591
  87.7 0.0 copy-start.2
  87.7 0.0 copy-start.3
  87.7 0.0 copy-start.4
  87.7 0.0 copy-start.5
  87.7 0.0 copy-done.6
  87.7 0.0 copy-done.7
  87.8 0.8 copy-done.2
  88.6 0.1 copy-done.3
  88.6 0.1 copy-done.4
  88.7 0.1 copy-done.5
  88.8 0.0 copy-start.1
  88.8 0.9 %subtract_convert_fusion = (bf16[2,64,256]{2,1,0:T(8,128)(2,1)}, f32[2,64,256]{2,1,0:T(8,128)}, f32[2,64,256]{2,1,0:T(8,128)}, bf16[2,64,256]{2,1,0:T(8,128)(2,1...) fusion(bf16[2,64,256]{2,1,0:T(8,128)(2,1)S(1)} %copy-done.7, f32[1,64,256]{2,1,0:T(8,128)S(1)} %get-tuple-element.21, ...), kind=kLoop, calls=%fused_computation.6 | loop fusion | flops 1048576 | bytes 1572864 | tf_op jit(solution)/shard_map/convert_element_type | solution.py:585
  89.7 0.3 copy-done.1
  90.0 0.0 copy-start
  90.0 0.8 copy.21
  90.8 0.4 copy-done
  91.2 0.8 copy.22
  (1 shorter events, 0.0 us)
Async XLA Ops:
  86.6 1.1 %copy-start.6 = (bf16[2,64,256]{2,1,0:T(8,128)(2,1)S(1)}, bf16[2,64,256]{2,1,0:T(8,128)(2,1)}, u32[]{:S(2)}) copy-start(bf16[2,64,256]{2,1,0:T(8,128)(2,1)} %fw_in.1) | copy-start | bytes 196612
  86.6 1.1 %copy-start.7 = (bf16[2,64,256]{2,1,0:T(8,128)(2,1)S(1)}, bf16[2,64,256]{2,1,0:T(8,128)(2,1)}, u32[]{:S(2)}) copy-start(bf16[2,64,256]{2,1,0:T(8,128)(2,1)} %gw_in.1) | copy-start | bytes 196612
  87.7 0.9 copy-start.2
  87.7 1.0 %copy-start.3 = (f32[2,64,256]{2,1,0:T(8,128)S(1)}, f32[2,64,256]{2,1,0:T(8,128)}, u32[]{:S(2)}) copy-start(f32[2,64,256]{2,1,0:T(8,128)} %param.18) | copy-start | bytes 393220
  87.7 1.0 %copy-start.4 = (f32[2,64,256]{2,1,0:T(8,128)S(1)}, f32[2,64,256]{2,1,0:T(8,128)}, u32[]{:S(2)}) copy-start(f32[2,64,256]{2,1,0:T(8,128)} %param.16) | copy-start | bytes 393220
  87.7 1.1 %copy-start.5 = (f32[2,64,256]{2,1,0:T(8,128)S(1)}, f32[2,64,256]{2,1,0:T(8,128)}, u32[]{:S(2)}) copy-start(f32[2,64,256]{2,1,0:T(8,128)} %param.15) | copy-start | bytes 393220
  88.8 1.2 %copy-start.1 = (bf16[128,2048]{1,0:T(8,128)(2,1)S(1)}, bf16[128,2048]{1,0:T(8,128)(2,1)}, u32[]{:S(2)}) copy-start(bf16[128,2048]{1,0:T(8,128)(2,1)} %get-tuple-element.11) | copy-start | bytes 1572868
  90.0 1.2 %copy-start = (bf16[128,2048]{1,0:T(8,128)(2,1)S(1)}, bf16[128,2048]{1,0:T(8,128)(2,1)}, u32[]{:S(2)}) copy-start(bf16[128,2048]{1,0:T(8,128)(2,1)} %get-tuple-element.12) | copy-start | bytes 1572868

commit v2 on v1

--- a/solution.py
+++ b/solution.py
@@ -19,11 +19,13 @@
 COLS = 256
 KB = 64
 PAD = 256
-CA = 512
+CA = 640
 CB = 4 * COLS - CA
 F32 = jnp.float32
 BF16 = jnp.bfloat16
 NSEM = 320
+VMEM_LIMIT = 62 * 2**20
+TR = 64
 MESH = pl.DeviceIdType.MESH
 
 
@@ -32,10 +34,10 @@
 
 
 def kernel(
-    dil_ref, x_in, ids_in, fw_in, gw_in, cot_in,
-    lay_out, dx_out, grad_out,
+    dil_ref, x_in, ids_in, fw_in, gw_in, fm_in, fv_in, gm_in, gv_in, cot_in,
+    lay_out, dx_out, fw_out, gw_out, fm_out, fv_out, gm_out, gv_out,
     xb, xt, wb, u0, u1, dl, dd, cotc, gcol, grow, cotv, idc, idr, idsrc,
-    dw, ra, za, rb, rbx, dxb, sib, yr, ssem, rsem, lsem,
+    gsum, dw, ra, za, rb, rbx, dxb, sib, yr, fm, fv, gm, gv, ssem, rsem, lsem,
 ):
     x, z = lax.axis_index("x"), lax.axis_index("z")
     y, c = lax.axis_index("y"), lax.axis_index("c")
@@ -92,6 +94,9 @@
         bring(gw_in.at[tap], wb.at[x, z, :, pl.ds(tap * 512 + COLS, COLS)])
     bring(x_in, rows_of(xb, me))
     bring(cot_in, cotv)
+    for src, dst in ((fm_in, fm), (fv_in, fv), (gm_in, gm), (gv_in, gv)):
+        bring(src, dst)
+    states = local[6:]
     idsrc[...] = jnp.broadcast_to(ids_in[...], (8, ROWS))
 
     barrier = pltpu.get_barrier_semaphore()
@@ -102,7 +107,7 @@
     for dev in peers:
         pl.semaphore_signal(barrier, inc=1, device_id=dev, device_id_type=MESH)
     pl.semaphore_wait(barrier, len(peers))
-    for copy in local:
+    for copy in local[:6]:
         copy.wait()
 
     def wa(xi, zi, lo=0, n=KB):
@@ -135,12 +140,22 @@
             arrived(("za", -1, r - 1), wa(x, at_z(r), 32, 32), ups)
 
     def x_send_a(r):
-        for k in (1, 2, 3):
+        for k in (1, 2, 3) if r == 4 else (1, 3):
             send(("xa", r, k), wa(x, at_z(r)), wa(x, at_z(r)), {"x": at_x(k)})
 
+    def x_relay_a(r):
+        for k, lo in ((1, 0), (3, 32)):
+            arrived(("xa", r, k), wa(at_x(-k), at_z(r)), {"x": at_x(-k)})
+            ref = wa(at_x(-k), at_z(r), lo, 32)
+            send(("xr", r, k), ref, ref, {"x": at_x(k)})
+
     def x_got_a(r):
-        for k in (1, 2, 3):
-            arrived(("xa", r, k), wa(at_x(-k), at_z(r)), {"x": at_x(-k)})
+        if r == 4:
+            for k in (1, 2, 3):
+                arrived(("xa", r, k), wa(at_x(-k), at_z(r)), {"x": at_x(-k)})
+        else:
+            for k, lo in ((1, 0), (3, 32)):
+                arrived(("xr", r, k), wa(at_x(2), at_z(r), lo, 32), {"x": at_x(-k)})
 
     def carried(direction, r):
         return (0, 1, 2, 3) if r < 4 else ((0, 1) if direction > 0 else (2, 3))
@@ -200,6 +215,7 @@
         z_send_b(0, 4 - k)
     z_got_b(1, 0)
     z_send_b(1, 0)
+    x_relay_a(0)
     transposed(me)
     arrived(("X", 1, 0), half(at_y(-1) * 2 + c, 0), {"y": at_y(-1)})
     send(("X", 1, 2), half(at_y(-1) * 2 + c, 0), half(at_y(-1) * 2 + c, 0), {"y": at_y(1)})
@@ -219,6 +235,8 @@
     for k in (3, 2, 1):
         z_got_b(1, k)
         z_send_b(1, k)
+    for r in (1, -1):
+        x_relay_a(r)
     arrived(("X", 1, 1), half(at_y(-1) * 2 + c, 1), {"y": at_y(-1)})
     send(("Xc", 1), rows_of(xb, at_y(-1) * 2 + c), rows_of(xb, at_y(-1) * 2 + c), {"c": oc})
     arrived(("X", -1, 1), half(at_y(1) * 2 + c, 0), {"y": at_y(1)})
@@ -236,6 +254,8 @@
     for k in (2, 1):
         z_got_b(2, k)
         z_send_b(2, k)
+    for r in (2, -2):
+        x_relay_a(r)
     z_got_a(4)
     x_send_a(4)
     arrived(("Xc", 1), rows_of(xb, at_y(-1) * 2 + oc), {"c": oc})
@@ -252,6 +272,8 @@
     for k in (2, 1):
         z_got_b(3, k)
         z_send_b(3, k)
+    for r in (3, -3):
+        x_relay_a(r)
     transposed(at_y(2) * 2 + c)
     for k, o in ctx_offsets:
         arrived(("id", k, o), idr.at[ctx_id(-k, o)], ctx_dev(-k, o))
@@ -303,28 +325,28 @@
     for k, o in ctx_offsets:
         arrived(("cot", k, o), rows_of(cotc, ctx_id(-k, o)), ctx_dev(-k, o))
 
-    @pl.loop(0, LEN // 128)
+    @pl.loop(0, LEN // TR)
     def _(i):
-        t0 = pl.multiple_of(i * 128, 128)
-        same = idc[pl.ds(PAD + t0, 128)] == idc[pl.ds(PAD + t0 - d, 128)]
+        t0 = pl.multiple_of(i * TR, TR)
+        same = idc[pl.ds(PAD + t0, TR)] == idc[pl.ds(PAD + t0 - d, TR)]
         for j in range(2):
             pre = []
             for part in range(2):
                 cols = pl.ds(part * COLS + j * 128, 128)
-                lag = u1[part * 2 + j, pl.ds(PAD + t0 - d, 128)]
-                pre.append(u0[pl.ds(t0, 128), cols] + jnp.where(same, lag, 0.0))
+                lag = u1[part * 2 + j, pl.ds(PAD + t0 - d, TR)]
+                pre.append(u0[pl.ds(t0, TR), cols] + jnp.where(same, lag, 0.0))
             f = jnp.tanh(pre[0])
-            g = jax.nn.sigmoid(pre[1])
+            g = 0.5 * jnp.tanh(0.5 * pre[1]) + 0.5
             near = pl.ds(j * 128, 128)
             far = pl.ds(COLS + j * 128, 128)
-            gcol[pl.ds(t0, 128), near] = (f * g).astype(BF16)
-            cot = cotc[pl.ds(t0, 128), near].astype(F32)
-            fd = (cot * g * (1.0 - f * f)).astype(BF16)
-            gd = (cot * f * g * (1.0 - g)).astype(BF16)
-            dd[pl.ds(t0, 128), near] = fd
-            dd[pl.ds(t0, 128), far] = gd
-            dl[j, pl.ds(t0, 128)] = fd.astype(F32)
-            dl[2 + j, pl.ds(t0, 128)] = gd.astype(F32)
+            gcol[pl.ds(t0, TR), near] = (f * g).astype(BF16)
+            cot = cotc[pl.ds(t0, TR), near].astype(F32) * g
+            fd = (cot * (1.0 - f * f)).astype(BF16)
+            gd = (cot * f * (1.0 - g)).astype(BF16)
+            dd[pl.ds(t0, TR), near] = fd
+            dd[pl.ds(t0, TR), far] = gd
+            dl[j, pl.ds(t0, TR)] = fd.astype(F32)
+            dl[2 + j, pl.ds(t0, TR)] = gd.astype(F32)
 
     for k, o in ctx_offsets:
         send(("gat", k, o), rows_of(gcol, ctx_id(k, o)), cols_of(grow, me), ctx_dev(k, o))
@@ -332,13 +354,13 @@
         rows = pl.ds(pl.multiple_of(me * ROWS + part * 64, 64), 64)
         grow[pl.ds(part * 64, 64), pl.ds(pl.multiple_of(me * COLS, COLS), COLS)] = gcol[rows]
 
-    @pl.loop(0, LEN // 128)
+    @pl.loop(0, LEN // TR)
     def _(i):
-        t0 = pl.multiple_of(i * 128, 128)
-        same = idc[pl.ds(PAD + t0, 128)] == idc[pl.ds(PAD + t0 + d, 128)]
+        t0 = pl.multiple_of(i * TR, TR)
+        same = idc[pl.ds(PAD + t0, TR)] == idc[pl.ds(PAD + t0 + d, TR)]
         for j in range(4):
-            ahead = dl[j, pl.ds(t0 + d, 128)]
-            dd[pl.ds(t0, 128), pl.ds(512 + j * 128, 128)] = jnp.where(same, ahead, 0.0).astype(BF16)
+            ahead = dl[j, pl.ds(t0 + d, TR)]
+            dd[pl.ds(t0, TR), pl.ds(512 + j * 128, 128)] = jnp.where(same, ahead, 0.0).astype(BF16)
 
     def grad_w(r):
         zi = at_z(r)
@@ -353,19 +375,36 @@
     def db(xi, zi):
         return dw.at[xi, zi, :, pl.ds(CA, CB)]
 
+    def direct(r):
+        return r in (4, 0)
+
     def sum_x_send(r):
-        for k in (1, 2, 3):
-            send(("sxa", r, k), da(at_x(k), at_z(r)), ra.at[k - 1, at_z(r)], {"x": at_x(k)})
+        zi = at_z(r)
+        if direct(r):
+            for k in (1, 2, 3):
+                send(("sxa", r, k), da(at_x(k), zi), ra.at[k - 1, zi], {"x": at_x(k)})
+        else:
+            for k, lo in ((1, 0), (3, 32)):
+                dst = ra.at[1, zi, pl.ds(lo, 32)]
+                send(("sxr", r, k), da(at_x(2), zi, lo, 32), dst, {"x": at_x(k)})
+
+    def sum_x_relay(r):
+        zi = at_z(r)
+        for k, lo in ((1, 0), (3, 32)):
+            rows = pl.ds(lo, 32)
+            arrived(("sxr", r, k), ra.at[1, zi, rows], {"x": at_x(-k)})
+            ref = da(at_x(k), zi, lo, 32)
+            ref[...] = (ref[...].astype(F32) + ra[1, zi, rows].astype(F32)).astype(BF16)
+            send(("sxa", r, k), da(at_x(k), zi), ra.at[k - 1, zi], {"x": at_x(k)})
 
     def sum_x_got(r):
-        for k in (1, 2, 3):
+        for k in (1, 2, 3) if direct(r) else (1, 3):
             arrived(("sxa", r, k), ra.at[k - 1, at_z(r)], {"x": at_x(-k)})
 
     def a_sum(r):
         zi = at_z(r)
-        return (da(x, zi)[...].astype(F32) + ra[0, zi].astype(F32)) + (
-            ra[1, zi].astype(F32) + ra[2, zi].astype(F32)
-        )
+        total = da(x, zi)[...].astype(F32) + ra[0, zi].astype(F32) + ra[2, zi].astype(F32)
+        return total + ra[1, zi].astype(F32) if direct(r) else total
 
     def a_far():
         sum_x_got(4)
@@ -408,7 +447,7 @@
         ref = db(at_x(k), z)
         total = ref[...].astype(F32) + (rb[0, 0, k].astype(F32) + rb[1, 0, k].astype(F32))
         if k == 0:
-            grad_out[:, pl.ds(CA, CB)] = total
+            gsum[:, pl.ds(CA, CB)] = total
         else:
             ref[...] = total.astype(BF16)
             send(("sxb", k), ref, rbx.at[k - 1], {"x": at_x(k)})
@@ -457,6 +496,48 @@
                 dxb[yi, c, some] = total.astype(BF16)
 
             send(("y", s, 1), dxb.at[yi, c], yr.at[h, 1], {"y": at_y(s)})
+
+    def adam(j):
+        tap, gate, cols = j // 4, (j // 2) % 2, pl.ds((j % 2) * 128, 128)
+        moment, second = ((fm, fv), (gm, gv))[gate]
+        outs = ((fw_out, fm_out, fv_out), (gw_out, gm_out, gv_out))[gate]
+        results = adam_update(
+            wb[x, z, :, pl.ds(j * 128, 128)],
+            moment[tap, :, cols],
+            second[tap, :, cols],
+            gsum[:, pl.ds(j * 128, 128)] * (1.0 / (LEN * NX * NZ)),
+        )
+        for out, result in zip(outs, results):
+            out[tap, :, cols] = result
+
+    def y_last():
+        pair_sum(0)
+        for s, h in ((1, 0), (-1, 1)):
+            arrived(("y", s, 1), yr.at[h, 1], {"y": at_y(-s)})
+
+        @pl.loop(0, 4)
+        def _(i):
+            rows = pl.ds(pl.multiple_of(i * 32, 32), 32)
+            far = yr[0, 1, rows].astype(F32) + yr[1, 1, rows].astype(F32)
+            back = dxb[y, c, rows].astype(F32) + far
+            dx_out[rows] = (cotv[rows].astype(F32) + back).astype(BF16)
+
+    def a_last():
+        sum_x_got(0)
+        total = a_sum(0)
+        for s, h, src in ((1, 0, downs), (-1, 1, ups)):
+            arrived(("sza", s, 1), za.at[h, 0], src)
+        gsum[:, pl.ds(0, CA)] = total + (za[0, 0].astype(F32) + za[1, 0].astype(F32))
+        for j in range(CA // 128):
+            adam(j)
+
+    def b_end():
+        for k in (1, 2, 3):
+            arrived(("sxb", k), rbx.at[k - 1], {"x": at_x(-k)})
+        across = rbx[0].astype(F32) + rbx[1].astype(F32) + rbx[2].astype(F32)
+        gsum[:, pl.ds(CA, CB)] += across
+        for j in range(CA // 128, 8):
+            adam(j)
 
     grad_w(4)
     sum_x_send(4)
@@ -467,29 +548,35 @@
     grad_w(-3)
     sum_x_send(-3)
     y_far()
-    for k in range(4):
-        b_step(3, k)
-    a_far()
-    grad_x(1)
     grad_w(2)
     sum_x_send(2)
     grad_w(-2)
     sum_x_send(-2)
+    for k in range(4):
+        b_step(3, k)
+    a_far()
+    for r in (3, -3):
+        sum_x_relay(r)
+    grad_x(1)
     grad_x(-1)
     for k in range(4):
         b_step(2, k)
-    a_step(3)
     y_step()
     grad_w(1)
     sum_x_send(1)
     grad_w(-1)
     sum_x_send(-1)
-    grad_w(0)
-    sum_x_send(0)
-    a_step(2)
-    grad_x(0)
+    for r in (2, -2):
+        sum_x_relay(r)
+    a_step(3)
     for k in range(4):
         b_step(1, k)
+    grad_w(0)
+    for r in (1, -1):
+        sum_x_relay(r)
+    sum_x_send(0)
+    grad_x(0)
+    a_step(2)
     for k, o in ctx_offsets:
         arrived(("gat", k, o), cols_of(grow, ctx_id(-k, o)), ctx_dev(-k, o))
 
@@ -499,33 +586,20 @@
         mine = xb[pl.ds(pl.multiple_of(me * ROWS + i * 32, 32), 32)]
         lay_out[rows] = (mine.astype(F32) + grow[rows].astype(F32)).astype(BF16)
 
-    pair_sum(0)
-    a_step(1)
     for k in (1, 2, 3, 0):
         b_last(k)
-    for s, h in ((1, 0), (-1, 1)):
-        arrived(("y", s, 1), yr.at[h, 1], {"y": at_y(-s)})
-
-    @pl.loop(0, 4)
-    def _(i):
-        rows = pl.ds(pl.multiple_of(i * 32, 32), 32)
-        back = dxb[y, c, rows].astype(F32) + (yr[0, 1, rows].astype(F32) + yr[1, 1, rows].astype(F32))
-        dx_out[rows] = (cotv[rows].astype(F32) + back).astype(BF16)
-
-    sum_x_got(0)
-    total = a_sum(0)
-    for s, h, src in ((1, 0, downs), (-1, 1, ups)):
-        arrived(("sza", s, 1), za.at[h, 0], src)
-    grad_out[:, pl.ds(0, CA)] = total + (za[0, 0].astype(F32) + za[1, 0].astype(F32))
-    for k in (1, 2, 3):
-        arrived(("sxb", k), rbx.at[k - 1], {"x": at_x(-k)})
-    grad_out[:, pl.ds(CA, CB)] += rbx[0].astype(F32) + rbx[1].astype(F32) + rbx[2].astype(F32)
+    a_step(1)
+    for copy in states:
+        copy.wait()
+    y_last()
+    b_end()
+    a_last()
     for copy in sent:
         copy.wait_send()
 
 
-def fused(dilation, inputs, ids, fw, gw, cot):
-    any_space = pl.BlockSpec(memory_space=pl.ANY)
+def fused(dilation, inputs, ids, fw, gw, fm, fv, gm, gv, cot):
+    hbm = pl.BlockSpec(memory_space=pltpu.HBM)
     vmem = pl.BlockSpec(memory_space=pltpu.VMEM)
     scratch = [
         ((LEN, CH), BF16),
@@ -542,6 +616,7 @@
         ((PAD + LEN + PAD, 128), jnp.int32),
         ((NY * NC, 8, ROWS), jnp.int32),
         ((8, ROWS), jnp.int32),
+        ((KB, 4 * COLS), F32),
         ((NX, NZ, KB, 4 * COLS), BF16),
         ((3, NZ, KB, CA), BF16),
         ((2, 4, KB, CA), BF16),
@@ -550,30 +625,44 @@
         ((NY, NC, ROWS, CH), BF16),
         ((NY, ROWS, CH), BF16),
         ((2, 2, ROWS, CH), BF16),
+        *[((2, KB, COLS), F32)] * 4,
     ]
+    rows = jax.ShapeDtypeStruct((ROWS, CH), BF16)
+    weight = jax.ShapeDtypeStruct((2, KB, COLS), BF16)
+    state = jax.ShapeDtypeStruct((2, KB, COLS), F32)
     return pl.pallas_call(
         kernel,
         name="layer",
-        out_shape=(
-            jax.ShapeDtypeStruct((ROWS, CH), BF16),
-            jax.ShapeDtypeStruct((ROWS, CH), BF16),
-            jax.ShapeDtypeStruct((KB, 4 * COLS), F32),
-        ),
-        in_specs=[
-            pl.BlockSpec(memory_space=pltpu.SMEM), any_space, vmem, any_space, any_space, any_space,
-        ],
-        out_specs=(vmem, vmem, vmem),
+        out_shape=(rows, rows, weight, weight, *[state] * 4),
+        in_specs=[pl.BlockSpec(memory_space=pltpu.SMEM), hbm, vmem, *[hbm] * 7],
+        out_specs=(vmem,) * 8,
         scratch_shapes=[pltpu.VMEM(s, t) for s, t in scratch]
         + [
             pltpu.SemaphoreType.DMA((NSEM,)),
             pltpu.SemaphoreType.DMA((NSEM,)),
-            pltpu.SemaphoreType.DMA((6,)),
+            pltpu.SemaphoreType.DMA((10,)),
         ],
         compiler_params=pltpu.CompilerParams(
-            collective_id=0, has_side_effects=True, vmem_limit_bytes=60 * 2**20
+            collective_id=0, has_side_effects=True, vmem_limit_bytes=VMEM_LIMIT
         ),
         cost_estimate=pl.CostEstimate(flops=13 * 10**9, bytes_accessed=2**23, transcendentals=2**20),
-    )(dilation, inputs, ids, fw, gw, cot)
+    )(dilation, inputs, ids, fw, gw, fm, fv, gm, gv, cot)
+
+
+def hand_over(*refs):
+    count = len(refs) // 2
+    for src, dst in zip(refs[:count], refs[count:]):
+        dst[...] = src[...]
+
+
+def placed(arrays):
+    return pl.pallas_call(
+        hand_over,
+        name="hand_over",
+        out_shape=tuple(jax.ShapeDtypeStruct(a.shape, a.dtype) for a in arrays),
+        in_specs=[pl.BlockSpec(memory_space=pltpu.VMEM)] * len(arrays),
+        out_specs=(pl.BlockSpec(memory_space=pltpu.VMEM),) * len(arrays),
+    )(*arrays)
 
 
 def adam_update(weight, moment, second, gradient):
@@ -587,13 +676,9 @@
 
 
 def per_device(inputs, doc_ids, dilation, fw, gw, fm, fv, gm, gv, cotangent):
-    layer_out, input_grad, grads = fused(dilation, inputs[0], doc_ids, fw, gw, cotangent[0])
-    grads = grads / (LEN * NX * NZ)
-    filter_grad = jnp.stack([grads[:, 0:256], grads[:, 512:768]])
-    gate_grad = jnp.stack([grads[:, 256:512], grads[:, 768:1024]])
-    new_fw, new_fm, new_fv = adam_update(fw, fm, fv, filter_grad)
-    new_gw, new_gm, new_gv = adam_update(gw, gm, gv, gate_grad)
-    return (layer_out[None], input_grad[None], new_fw, new_gw, new_fm, new_fv, new_gm, new_gv)
+    results = fused(dilation, inputs[0], doc_ids, fw, gw, fm, fv, gm, gv, cotangent[0])
+    layer_out, input_grad, *states = placed(results)
+    return (layer_out[None], input_grad[None], *states)
 
 
 def solution(mesh):

time: 93 us -> 86.2 us (0.927)
  local copies, waits for them, and re-layouts: 3.34 us -> 0 us
  Pallas kernels: 85.3 us -> 83.2 us
  other arithmetic: 1.95 us -> 0 us
    unnamed x18 -> x0, local copies, waits for them, and re-layouts: 3.32 us -> none
    pallas_call x1 -> x2, Pallas kernels: 85.3 us -> 83.2 us  [the longest x1 80.6 us: fused(): pl.pallas_call(kernel, name='layer', out_shape=(rows, rows, weight, weigh...]
    div x1 -> x0, other arithmetic: 1 us -> none  [per_device(): grads = grads / (LEN * NX * NZ)]
    convert_element_type x1 -> x0, other arithmetic: 0.94 us -> none  [adam_update(): new_weight = (weight.astype(F32) - LEARN_RATE * step_size).astype(BF16)]
where the time goes in v2:
time: 86.2 us; the launch traced here: 84.5 us
  Pallas kernels  83.2 us (97%)
  between operations  1.29 us (1%)
    pallas_call x1, Pallas kernels, fused(): pl.pallas_call(kernel, name='layer', out_shape=(rows, rows, weight, weigh...  80.6 us
    pallas_call x1, Pallas kernels, placed(): pl.pallas_call(hand_over, name='hand_over', out_shape=tuple((jax.ShapeDty...  2.59 us

profile of v2, /device:TPU:2, one launch (start us, length us, event | category | flops | bytes accessed | tf_op | source)
XLA Modules:
  0.0 84.5 jit_solution(12463694016396626404)
XLA Ops:
  1.3 80.6 %layer.1 = (bf16[128,2048]{1,0:T(8,128)(2,1)}, bf16[128,2048]{1,0:T(8,128)(2,1)}, bf16[2,64,256]{2,1,0:T(8,128)(2,1)}, bf16[2,64,256]{2,1,0:T(8,128)(2,1)}, f32[...) custom-call(s32[1]{0:T(128)S(6)} %copy.18.dil_ref, ...), custom_call_target="tpu_custom_call" | custom-call | flops 12999999488 | bytes 8388608 | tf_op jit(solution)/shard_map/layer/pallas_call | solution.py:633
  81.9 2.6 %hand_over.1 = (bf16[128,2048]{1,0:T(8,128)(2,1)}, bf16[128,2048]{1,0:T(8,128)(2,1)}, bf16[2,64,256]{2,1,0:T(8,128)(2,1)}, bf16[2,64,256]{2,1,0:T(8,128)(2,1)}, ...) custom-call(bf16[128,2048]{1,0:T(8,128)(2,1)} %get-tuple-element.24.refs_0_, ...), custom_call_target="tpu_custom_call" | custom-call | tf_op jit(solution)/shard_map/hand_over/pallas_call | solution.py:659

commit v3 on v2

--- a/solution.py
+++ b/solution.py
@@ -232,11 +232,11 @@
         cotc[rows] = cotv[pl.ds(part * 64, 64), pl.ds(pl.multiple_of(me * COLS, COLS), COLS)]
     arrived(("Xc", 0), rows_of(xb, y * 2 + oc), {"c": oc})
     transposed(y * 2 + oc)
+    for r in (1, -1):
+        x_relay_a(r)
     for k in (3, 2, 1):
         z_got_b(1, k)
         z_send_b(1, k)
-    for r in (1, -1):
-        x_relay_a(r)
     arrived(("X", 1, 1), half(at_y(-1) * 2 + c, 1), {"y": at_y(-1)})
     send(("Xc", 1), rows_of(xb, at_y(-1) * 2 + c), rows_of(xb, at_y(-1) * 2 + c), {"c": oc})
     arrived(("X", -1, 1), half(at_y(1) * 2 + c, 0), {"y": at_y(1)})
@@ -250,12 +250,12 @@
     transposed(at_y(-1) * 2 + c)
     z_got_b(2, 3)
     z_send_b(2, 3)
+    for r in (2, -2):
+        x_relay_a(r)
     transposed(at_y(1) * 2 + c)
     for k in (2, 1):
         z_got_b(2, k)
         z_send_b(2, k)
-    for r in (2, -2):
-        x_relay_a(r)
     z_got_a(4)
     x_send_a(4)
     arrived(("Xc", 1), rows_of(xb, at_y(-1) * 2 + oc), {"c": oc})
@@ -266,14 +266,14 @@
     z_send_b(3, 0)
     z_got_b(3, 3)
     z_send_b(3, 3)
+    for r in (3, -3):
+        x_relay_a(r)
     arrived(("X", 1, 2), half(at_y(2) * 2 + c, 0), {"y": at_y(-1)})
     arrived(("X", -1, 2), half(at_y(2) * 2 + c, 1), {"y": at_y(1)})
     send(("Xc", 3), rows_of(xb, at_y(2) * 2 + c), rows_of(xb, at_y(2) * 2 + c), {"c": oc})
     for k in (2, 1):
         z_got_b(3, k)
         z_send_b(3, k)
-    for r in (3, -3):
-        x_relay_a(r)
     transposed(at_y(2) * 2 + c)
     for k, o in ctx_offsets:
         arrived(("id", k, o), idr.at[ctx_id(-k, o)], ctx_dev(-k, o))
@@ -287,10 +287,10 @@
     transposed(at_y(2) * 2 + oc)
 
     def forward(pair, first):
-        @pl.loop(0, 4)
+        @pl.loop(0, 1)
         def _(i):
-            rows = pl.ds(pl.multiple_of(i * 256, 256), 256)
-            lags = pl.ds(pl.multiple_of(PAD + i * 256, 256), 256)
+            rows = pl.ds(pl.multiple_of(i * 1024, 512), 1024)
+            lags = pl.ds(pl.multiple_of(PAD + i * 1024, 256), 1024)
             lhs = jnp.concatenate(
                 [
                     xb[rows, pl.ds(pl.multiple_of(xi * 512 + pair * 128, 128), 128)]
@@ -362,12 +362,14 @@
             ahead = dl[j, pl.ds(t0 + d, TR)]
             dd[pl.ds(t0, TR), pl.ds(512 + j * 128, 128)] = jnp.where(same, ahead, 0.0).astype(BF16)
 
-    def grad_w(r):
-        zi = at_z(r)
+    def grad_w(*steps):
         for part in range(2):
-            lhs = xt[:, zi].reshape(NX * KB, LEN)
-            out = jnp.dot(lhs, dd[:, pl.ds(part * 512, 512)], preferred_element_type=F32)
-            dw[:, zi, :, pl.ds(part * 512, 512)] = out.astype(BF16).reshape(NX, KB, 512)
+            cols = pl.ds(part * 512, 512)
+            lhs = [xt[:, at_z(r)].reshape(NX * KB, LEN) for r in steps]
+            out = jnp.dot(jnp.concatenate(lhs, axis=0), dd[:, cols], preferred_element_type=F32)
+            for i, r in enumerate(steps):
+                mine = out[i * 256 : i * 256 + 256].astype(BF16)
+                dw[:, at_z(r), :, cols] = mine.reshape(NX, KB, 512)
 
     def da(xi, zi, lo=0, n=KB):
         return dw.at[xi, zi, pl.ds(lo, n), pl.ds(0, CA)]
@@ -376,7 +378,7 @@
         return dw.at[xi, zi, :, pl.ds(CA, CB)]
 
     def direct(r):
-        return r in (4, 0)
+        return r == 4
 
     def sum_x_send(r):
         zi = at_z(r)
@@ -543,38 +545,36 @@
     sum_x_send(4)
     b_far()
     grad_x(2)
-    grad_w(3)
+    grad_w(3, -3)
     sum_x_send(3)
-    grad_w(-3)
     sum_x_send(-3)
-    y_far()
     grad_w(2)
     sum_x_send(2)
+    for k in range(4):
+        b_step(3, k)
     grad_w(-2)
     sum_x_send(-2)
-    for k in range(4):
-        b_step(3, k)
     a_far()
+    y_far()
+    grad_x(1)
     for r in (3, -3):
         sum_x_relay(r)
-    grad_x(1)
-    grad_x(-1)
+    grad_w(1, -1)
+    sum_x_send(1)
+    sum_x_send(-1)
     for k in range(4):
         b_step(2, k)
-    y_step()
-    grad_w(1)
-    sum_x_send(1)
-    grad_w(-1)
-    sum_x_send(-1)
     for r in (2, -2):
         sum_x_relay(r)
+    grad_x(-1)
+    grad_w(0)
+    sum_x_send(0)
     a_step(3)
+    y_step()
     for k in range(4):
         b_step(1, k)
-    grad_w(0)
-    for r in (1, -1):
+    for r in (1, -1, 0):
         sum_x_relay(r)
-    sum_x_send(0)
     grad_x(0)
     a_step(2)
     for k, o in ctx_offsets:

time: 86.2 us -> 82.5 us (0.957)
  Pallas kernels: 83.2 us -> 80.3 us
    pallas_call x1, Pallas kernels: 80.6 us -> 77.7 us  [fused(): pl.pallas_call(kernel, name='layer', out_shape=(rows, rows, weight, weigh...]
where the time goes in v3:
time: 82.5 us; the launch traced here: 81.6 us
  Pallas kernels  80.3 us (97%)
  between operations  1.29 us (2%)
    pallas_call x1, Pallas kernels, fused(): pl.pallas_call(kernel, name='layer', out_shape=(rows, rows, weight, weigh...  77.7 us
    pallas_call x1, Pallas kernels, placed(): pl.pallas_call(hand_over, name='hand_over', out_shape=tuple((jax.ShapeDty...  2.59 us

profile of v3, /device:TPU:2, one launch (start us, length us, event | category | flops | bytes accessed | tf_op | source)
XLA Modules:
  0.0 81.6 jit_solution(8533979865756476363)
XLA Ops:
  1.3 77.7 %layer.1 = (bf16[128,2048]{1,0:T(8,128)(2,1)}, bf16[128,2048]{1,0:T(8,128)(2,1)}, bf16[2,64,256]{2,1,0:T(8,128)(2,1)}, bf16[2,64,256]{2,1,0:T(8,128)(2,1)}, f32[...) custom-call(s32[1]{0:T(128)S(6)} %copy.18.dil_ref, ...), custom_call_target="tpu_custom_call" | custom-call | flops 12999999488 | bytes 8388608 | tf_op jit(solution)/shard_map/layer/pallas_call | solution.py:633
  79.0 2.6 %hand_over.1 = (bf16[128,2048]{1,0:T(8,128)(2,1)}, bf16[128,2048]{1,0:T(8,128)(2,1)}, bf16[2,64,256]{2,1,0:T(8,128)(2,1)}, bf16[2,64,256]{2,1,0:T(8,128)(2,1)}, ...) custom-call(bf16[128,2048]{1,0:T(8,128)(2,1)} %get-tuple-element.24.refs_0_, ...), custom_call_target="tpu_custom_call" | custom-call | tf_op jit(solution)/shard_map/hand_over/pallas_call | solution.py:659

commit v4 on v3

--- a/solution.py
+++ b/solution.py
@@ -93,10 +93,6 @@
         bring(fw_in.at[tap], wb.at[x, z, :, pl.ds(tap * 512, COLS)])
         bring(gw_in.at[tap], wb.at[x, z, :, pl.ds(tap * 512 + COLS, COLS)])
     bring(x_in, rows_of(xb, me))
-    bring(cot_in, cotv)
-    for src, dst in ((fm_in, fm), (fv_in, fv), (gm_in, gm), (gv_in, gv)):
-        bring(src, dst)
-    states = local[6:]
     idsrc[...] = jnp.broadcast_to(ids_in[...], (8, ROWS))
 
     barrier = pltpu.get_barrier_semaphore()
@@ -107,7 +103,7 @@
     for dev in peers:
         pl.semaphore_signal(barrier, inc=1, device_id=dev, device_id_type=MESH)
     pl.semaphore_wait(barrier, len(peers))
-    for copy in local[:6]:
+    for copy in local[:4]:
         copy.wait()
 
     def wa(xi, zi, lo=0, n=KB):
@@ -174,6 +170,7 @@
     z_send_a(0)
     for k in (1, 2, 3):
         send(("xb", k), wbp(x, z), wbp(x, z), {"x": at_x(k)})
+    local[4].wait()
     for s, h in ((1, 0), (-1, 1)):
         send(("X", s, 0), half(me, h), half(me, h), {"y": at_y(s)})
     send(("Xc", 0), rows_of(xb, me), rows_of(xb, me), {"c": oc})
@@ -192,6 +189,10 @@
     for k, o in ctx_offsets:
         send(("id", k, o), idsrc, idr.at[me], ctx_dev(k, o))
 
+    bring(cot_in, cotv)
+    for src, dst in ((fm_in, fm), (fv_in, fv), (gm_in, gm), (gv_in, gv)):
+        bring(src, dst)
+    states = local[6:]
     idr[me] = idsrc[...]
     idc[pl.ds(0, PAD)] = jnp.full((PAD, 128), -1, jnp.int32)
     idc[pl.ds(PAD + LEN, PAD)] = jnp.full((PAD, 128), -2, jnp.int32)
@@ -225,6 +226,7 @@
     z_send_a(2)
     for r in (2, -2):
         x_send_a(r)
+    local[5].wait()
     for k, o in ctx_offsets:
         send(("cot", k, o), cols_of(cotv, ctx_id(k, o)), rows_of(cotc, me), ctx_dev(k, o))
     for part in range(2):

time: 82.5 us -> 82.5 us (level)
  no operation moved by 1% of the time
where the time goes in v4:
time: 82.5 us; the launch traced here: 81.7 us
  Pallas kernels  80.4 us (97%)
  between operations  1.29 us (2%)
    pallas_call x1, Pallas kernels, fused(): pl.pallas_call(kernel, name='layer', out_shape=(rows, rows, weight, weigh...  77.8 us
    pallas_call x1, Pallas kernels, placed(): pl.pallas_call(hand_over, name='hand_over', out_shape=tuple((jax.ShapeDty...  2.59 us

profile of v4, /device:TPU:2, one launch (start us, length us, event | category | flops | bytes accessed | tf_op | source)
XLA Modules:
  0.0 81.7 jit_solution(129928387360715476)
XLA Ops:
  1.3 77.8 %layer.1 = (bf16[128,2048]{1,0:T(8,128)(2,1)}, bf16[128,2048]{1,0:T(8,128)(2,1)}, bf16[2,64,256]{2,1,0:T(8,128)(2,1)}, bf16[2,64,256]{2,1,0:T(8,128)(2,1)}, f32[...) custom-call(s32[1]{0:T(128)S(6)} %copy.18.dil_ref, ...), custom_call_target="tpu_custom_call" | custom-call | flops 12999999488 | bytes 8388608 | tf_op jit(solution)/shard_map/layer/pallas_call | solution.py:635
  79.1 2.6 %hand_over.1 = (bf16[128,2048]{1,0:T(8,128)(2,1)}, bf16[128,2048]{1,0:T(8,128)(2,1)}, bf16[2,64,256]{2,1,0:T(8,128)(2,1)}, bf16[2,64,256]{2,1,0:T(8,128)(2,1)}, ...) custom-call(bf16[128,2048]{1,0:T(8,128)(2,1)} %get-tuple-element.24.refs_0_, ...), custom_call_target="tpu_custom_call" | custom-call | tf_op jit(solution)/shard_map/hand_over/pallas_call | solution.py:661
